TPU v7x, 32 devices: a whole 2x2x4 slice. The times are simulated.
32 devices in a mesh: fibre: 16 (over z, x, core), freq: 2 (over y).
Axes of the slice: x: 2, y: 2, z: 4, core: 2. Of those that a mesh axis runs over, the one named last changes fastest.
Arguments:
- traces: bfloat16 [2, 1024, 4096], P(None, 'fibre'), may hold values from -50 to 50, as said below
- live: int32 [1024], P('fibre'), may hold values 0 or 1
- reach: int32 [16], P('fibre'), may hold values from 1 to 8
Outputs:
- correlations: float32 [16, 8, 64, 64, 128], P('fibre', 'freq')
Inputs may be any that keep to these rules, and one draw needn't show every extreme that they name: `traces`: records of the fibre's channels.
All inputs are finite; a program needn't handle non-finite values. No bound on the sum of `live` on one device may be relied on, other than what follows from the above.
Results may differ from a plain program's by a relative error of at most 0.0057.
Values may be sent and summed in bfloat16 or wider, within the bound.
No kernel may reach another device: no remote copies, remote signals or barrier semaphores. Data moves between devices by JAX's collectives and lax.ppermute only.
A program may use at most 64 MiB of HBM per device.

v0:
```python
import functools
import math

import jax
import jax.numpy as jnp
import ml_dtypes
import numpy as np
from jax import lax
from jax.experimental import pallas as pl
from jax.experimental.pallas import tpu as pltpu
from jax.sharding import PartitionSpec as P

BAND = 64
OFF = 8
LAGS = 128
VMEM_LIMIT = 56 * 1024 * 1024


def leak_spectrum(freqs, samples, window, shift, slots, period):
    steps = np.arange(window)
    tone = np.exp(2j * np.pi * ((freqs[:, None] * (steps - shift)[None]) % samples) / samples)
    bins = np.exp(-2j * np.pi * ((steps[:, None] * slots[None]) % period) / period)
    return tone @ bins


@functools.lru_cache(maxsize=None)
def build_tables(samples):
    width = LAGS
    residues = samples // width
    groups = residues // 2
    half = width // 2
    per_band = BAND // residues
    order = np.concatenate([np.arange(i, half, per_band) for i in range(per_band)])
    steps = np.arange(width)
    slots = np.arange(width + 1)
    forward = np.zeros((groups, 2 * width, 4 * half))
    to_bins = np.zeros((2, groups, 4 * half, 4, width))
    root = 1.0 / math.sqrt(2.0)
    re_a, im_a, re_b, im_b = (slice(i * half, (i + 1) * half) for i in range(4))
    for g in range(groups):
        freq_a = g + residues * order
        freq_b = (residues - g if g else groups) + residues * order
        wave_a = np.exp(-2j * np.pi * ((steps[:, None] * freq_a[None]) % samples) / samples)
        wave_b = np.exp(-2j * np.pi * ((steps[:, None] * freq_b[None]) % samples) / samples)
        top, low = forward[g, :width], forward[g, width:]
        top[:, re_a], top[:, im_a] = wave_a.real, wave_a.imag
        if g == 0:
            low[:, re_b], low[:, im_b] = wave_b.real, wave_b.imag
        else:
            low[:, re_a], low[:, im_a] = -wave_a.imag, wave_a.real
            top[:, re_b], top[:, im_b] = wave_b.real, wave_b.imag
            low[:, re_b], low[:, im_b] = wave_b.imag, -wave_b.real
        for side in range(2):
            window, shift = ((width, 0), (2 * width, half))[side]
            leak = functools.partial(
                leak_spectrum, samples=samples, window=window, shift=shift, slots=slots, period=2 * width
            )
            pos_a, neg_a, pos_b, neg_b = leak(freq_a), leak(-freq_a), leak(freq_b), leak(-freq_b)
            spec = np.zeros((2, 4 * half, width + 1), complex)
            if g == 0:
                zero = (freq_a == 0)[:, None]
                spec[0, re_a] = np.where(zero, pos_a, root * (pos_a + neg_a))
                spec[0, im_a] = np.where(zero, 0.0, root * 1j * (pos_a - neg_a))
                spec[1, re_b] = root * (pos_b + neg_b)
                spec[1, im_b] = root * 1j * (pos_b - neg_b)
            else:
                spec[0, re_a], spec[0, im_a] = root * pos_a, root * 1j * pos_a
                spec[0, re_b], spec[0, im_b] = root * neg_b, -root * 1j * neg_b
                spec[1, re_b], spec[1, im_b] = root * pos_b, root * 1j * pos_b
                spec[1, re_a], spec[1, im_a] = root * neg_a, -root * 1j * neg_a
            table = to_bins[side, g]
            table[:, 0], table[:, 1] = spec[0, :, :width].real, spec[0, :, :width].imag
            table[:, 2], table[:, 3] = spec[1, :, :width].real, spec[1, :, :width].imag
            if g == 0:
                ends = (spec[0, :, 0].real, spec[1, :, 0].real, spec[0, :, width].real, spec[1, :, width].real)
            else:
                ends = tuple(
                    math.sqrt(2.0) * v
                    for v in (spec[0, :, 0].real, spec[0, :, 0].imag, spec[0, :, width].real, spec[0, :, width].imag)
                )
            for q in range(4):
                table[:, q, 0] = ends[q]
    lags = np.arange(LAGS)
    phase = 2 * np.pi * ((steps[:, None] * lags[None]) % (2 * width)) / (2 * width)
    lag = np.stack([2 * np.cos(phase), -2 * np.sin(phase)])
    lag[0, 0], lag[1, 0] = 1.0, (-1.0) ** lags
    bf16 = ml_dtypes.bfloat16
    forward_t = forward.transpose(0, 2, 1)
    forward_hi = forward_t.astype(bf16)
    forward_lo = (forward_t - forward_hi.astype(np.float64)).astype(bf16)
    bins_t = to_bins.transpose(0, 1, 3, 4, 2).reshape(2, groups, 4 * width, 4 * half).astype(bf16)
    lag_t = lag.reshape(2 * width, LAGS).T.astype(bf16)
    scale = residues / (2.0 * width * samples) / math.sqrt(samples)
    return forward_hi, forward_lo, bins_t, lag_t, scale


def real_dft(values):
    n = len(values)
    if n == 2:
        return [(values[0] + values[1], None), (values[0] - values[1], None)]
    even, odd = real_dft(values[0::2]), real_dft(values[1::2])
    out = [None] * (n // 2 + 1)
    for k in range(n // 4 + 1):
        (er, ei), (pr, pi) = even[k], odd[k]
        angle = -2.0 * math.pi * k / n
        c, s = math.cos(angle), math.sin(angle)
        if k == 0:
            out[0] = (er + pr, None)
            out[n // 2] = (er - pr, None)
            continue
        if 4 * k == n:
            out[k] = (er, -pr)
            continue
        if pi is None:
            tr, ti = pr * c, pr * s
        elif 8 * k == n:
            tr, ti = (pr + pi) * c, (pi - pr) * c
        else:
            tr, ti = pr * c - pi * s, pr * s + pi * c
        if ei is None:
            out[k] = (er + tr, ti)
            out[n // 2 - k] = (er - tr, ti)
        else:
            out[k] = (er + tr, ei + ti)
            out[n // 2 - k] = (er - tr, ti - ei)
    return out


def prepare_kernel(own, first_ref, second_ref, fhi_hbm, flo_hbm, bins_hbm, out_ref,
                   fhi, flo, bins, yhi, ylo, spec, wide, sems):
    windows, channels, samples = first_ref.shape
    width = LAGS
    residues = samples // width
    groups = residues // 2
    rows = 2 * windows * channels
    lanes = 2 * channels
    depth = windows * groups * 4
    copies = [
        pltpu.make_async_copy(src, dst, sems.at[i])
        for i, (src, dst) in enumerate(((fhi_hbm, fhi), (flo_hbm, flo), (bins_hbm, bins)))
    ]
    for copy in copies:
        copy.start()

    step = 16
    per_window = channels // step

    def split(value):
        high = value.astype(jnp.bfloat16)
        return high, (value - high.astype(jnp.float32)).astype(jnp.bfloat16)

    def transform(n, carry):
        w, c = n // per_window, n % per_window
        for which, ref in enumerate((first_ref, second_ref)):
            if own and which:
                continue
            block = ref[w, pl.ds(pl.multiple_of(c * step, step), step), :].astype(jnp.float32)
            terms = real_dft([block[:, a * width:(a + 1) * width] for a in range(residues)])
            for g in range(groups):
                if g == 0:
                    parts = (terms[0][0], terms[groups][0])
                else:
                    parts = terms[g]
                for side, part in enumerate(parts):
                    hi, lo = split(part)
                    for copy_to in ((0, 1) if own else (which,)):
                        row = pl.multiple_of(w * lanes + copy_to * channels + c * step, step)
                        yhi[g, pl.ds(row, step), side * width:(side + 1) * width] = hi
                        ylo[g, pl.ds(row, step), side * width:(side + 1) * width] = lo
        return carry

    lax.fori_loop(0, windows * per_window, transform, 0)
    copies[0].wait()
    copies[1].wait()
    nt = (((1,), (1,)), ((), ()))
    bands = (samples // 2) // BAND

    def forward(g, power):
        value = lax.dot_general(fhi[g], yhi[g], nt, preferred_element_type=jnp.float32)
        value += lax.dot_general(flo[g], yhi[g], nt, preferred_element_type=jnp.float32)
        value += lax.dot_general(fhi[g], ylo[g], nt, preferred_element_type=jnp.float32)
        spec[g] = value
        squared = (value * value).reshape(2 * width // bands, bands, rows)
        return power + squared.sum(0)

    power = lax.fori_loop(0, groups, forward, jnp.zeros((bands, rows), jnp.float32), unroll=4)
    gain = 1.0 / jnp.sqrt(power * (1.0 / BAND) + 1e-6)
    copies[2].wait()

    def to_bins(g, carry):
        white = (spec[g].reshape(2 * width // bands, bands, rows) * gain[None]).reshape(2 * width, rows)
        value = jnp.dot(bins[g], white.astype(jnp.bfloat16), preferred_element_type=jnp.float32)
        parts = [value[q * width:(q + 1) * width] for q in range(4)]
        if own:
            left = lax.broadcasted_iota(jnp.int32, (width, rows), 1) % lanes < channels
            ends = lax.broadcasted_iota(jnp.int32, (width, rows), 0) == 0
            turned = [parts[1], -parts[0], parts[3], -parts[2]]
            zero = jnp.zeros_like(parts[0])
            real = [parts[q] if q < 2 else jnp.where(ends, zero, parts[q]) for q in range(4)]
            imag = [jnp.where(ends, zero if q < 2 else parts[q], turned[q]) for q in range(4)]
            parts = [jnp.where(left, real[q], imag[q]) for q in range(4)]
        for q in range(4):
            for w in range(windows):
                start = w * (groups * 4) + g * 4 + q
                wide[pl.ds(start, width, stride=depth + 1), :] = parts[q][:, w * lanes:(w + 1) * lanes]
        return carry

    lax.fori_loop(0, groups, to_bins, 0, unroll=4)
    def narrow(k, carry):
        block = wide[pl.ds(k * (depth + 1), depth), :]
        out_ref[k] = (block.T if own else block).astype(jnp.bfloat16)
        return carry

    lax.fori_loop(0, width, narrow, 0, unroll=8)


def prepare(first, second, tables, own):
    windows, channels, samples = first.shape
    forward_hi, forward_lo, bins_t = tables
    width = LAGS
    groups = samples // width // 2
    rows = 2 * windows * channels
    depth = windows * groups * 4
    lanes = 2 * channels
    shape = (width, lanes, depth) if own else (width, depth, lanes)
    any_spec = pl.BlockSpec(memory_space=pl.ANY)
    vmem_spec = pl.BlockSpec(memory_space=pltpu.VMEM)
    flops = 2 * groups * rows * (3 * 4 * width * width + 8 * width * width)
    return pl.pallas_call(
        functools.partial(prepare_kernel, own),
        out_shape=jax.ShapeDtypeStruct(shape, jnp.bfloat16),
        in_specs=[vmem_spec, vmem_spec, any_spec, any_spec, any_spec],
        out_specs=vmem_spec,
        scratch_shapes=[
            pltpu.VMEM(forward_hi.shape, jnp.bfloat16),
            pltpu.VMEM(forward_lo.shape, jnp.bfloat16),
            pltpu.VMEM(bins_t.shape, jnp.bfloat16),
            pltpu.VMEM((groups, rows, 2 * width), jnp.bfloat16),
            pltpu.VMEM((groups, rows, 2 * width), jnp.bfloat16),
            pltpu.VMEM((groups, 2 * width, rows), jnp.float32),
            pltpu.VMEM((width * (depth + 1), lanes), jnp.float32),
            pltpu.SemaphoreType.DMA((3,)),
        ],
        compiler_params=pltpu.CompilerParams(vmem_limit_bytes=VMEM_LIMIT),
        cost_estimate=pl.CostEstimate(flops=flops, bytes_accessed=14 * 2**20, transcendentals=0),
        name="prepare_own" if own else "prepare_partners",
    )(first, second, forward_hi, forward_lo, bins_t)


def stack_kernel(chunks, per_chunk, per_out, own_ref, first_ref, second_ref, lag_ref, slot_ref, keep_ref, out_ref, *cross):
    step = pl.program_id(0)
    width = LAGS
    lanes = first_ref.shape[2]
    channels = lanes // 2

    @pl.when(step < chunks)
    def _():
        def one(n, carry):
            k = step * per_chunk + n
            partners = jnp.concatenate([first_ref[n], second_ref[n]], axis=1)
            value = jnp.dot(own_ref[n], partners, preferred_element_type=jnp.float32)
            for side in range(2):
                for part in range(2):
                    cross[side][pl.ds(part * width + k, channels, stride=2 * width + 1), :] = (
                        value[part * channels:(part + 1) * channels, side * lanes:(side + 1) * lanes]
                    )
            return carry

        lax.fori_loop(0, per_chunk, one, 0, unroll=8)

    @pl.when(step >= chunks)
    def _():
        def one(n, carry):
            i = (step - chunks) * per_out + n
            part = pl.ds(i * (2 * width + 1), 2 * width)
            block = jnp.concatenate([ref[part, :].astype(jnp.bfloat16) for ref in cross], axis=1)
            value = jnp.dot(lag_ref[...], block, preferred_element_type=jnp.float32).T
            for o in range(out_ref.shape[0]):
                out_ref[slot_ref[o], n] = value[o * channels:(o + 1) * channels] * keep_ref[o]
            return carry

        lax.fori_loop(0, per_out, one, 0, unroll=4)


def stack(own, first, second, lag_t, slots, keep):
    width, lanes, depth = own.shape
    channels = lanes // 2
    chunks, out_chunks = 4, 8
    per_chunk, per_out = width // chunks, channels // out_chunks
    block = lambda s: (jnp.minimum(s, chunks - 1), 0, 0)
    offsets = keep.shape[0]
    return pl.pallas_call(
        functools.partial(stack_kernel, chunks, per_chunk, per_out),
        grid=(chunks + out_chunks,),
        out_shape=jax.ShapeDtypeStruct((offsets, channels, channels, LAGS), jnp.float32),
        in_specs=[
            pl.BlockSpec((per_chunk, lanes, depth), block),
            pl.BlockSpec((per_chunk, depth, lanes), block),
            pl.BlockSpec((per_chunk, depth, lanes), block),
            pl.BlockSpec(lag_t.shape, lambda s: (0, 0)),
            pl.BlockSpec(memory_space=pltpu.SMEM),
            pl.BlockSpec(memory_space=pltpu.SMEM),
        ],
        out_specs=pl.BlockSpec(
            (offsets, per_out, channels, LAGS), lambda s: (0, jnp.maximum(s - chunks, 0), 0, 0)
        ),
        scratch_shapes=[pltpu.VMEM((channels * (2 * width + 1), lanes), jnp.float32)] * 2,
        compiler_params=pltpu.CompilerParams(
            vmem_limit_bytes=VMEM_LIMIT, dimension_semantics=("arbitrary",)
        ),
        name="stack_lags",
    )(own, first, second, lag_t, slots, keep)


def per_device(traces, live, reach):
    windows, channels, samples = traces.shape
    blocks = lax.axis_size("fibre")
    splits = lax.axis_size("freq")
    owned = OFF // splits
    place = lax.axis_index("freq")
    forward_hi, forward_lo, bins_t, lag_t, scale = build_tables(samples)
    forward_hi, forward_lo = jnp.asarray(forward_hi), jnp.asarray(forward_lo)
    masked = traces * live.astype(traces.dtype)[None, :, None]

    quads = blocks // owned
    half = owned // 2
    u = lax.axis_index("fibre") % owned
    core, pair = u % half, u // half

    def rank(q, pair, core, part):
        return (q * owned + pair * half + core) * splits + part

    def send(payload, route):
        pairs = []
        for q in range(quads):
            for p in range(2):
                for c in range(half):
                    for g in range(splits):
                        source = route(q, p, c, g)
                        if source[0] < quads:
                            pairs.append((rank(*source), rank(q, p, c, g)))
        return lax.ppermute(payload, ("fibre", "freq"), pairs)

    upper = send(masked, lambda q, p, c, g: (q + 1, p, c, g))
    own = prepare(masked, masked, (forward_hi, forward_lo, jnp.asarray(bins_t[1])), True)
    upper, own = lax.optimization_barrier((upper, own))
    core_payload = jnp.where((core == 1) & (place == 0), masked, upper)
    across_payload = jnp.where((pair == 1) & (place == 0), masked, upper)
    beside = send(core_payload, lambda q, p, c, g: (q + c * g, p, 1 - c, 1 - g if c else g))
    across = send(across_payload, lambda q, p, c, g: (q + p * g, 1 - p, c, g))
    here = jnp.where(place == 0, masked, upper)
    partner_tables = (forward_hi, forward_lo, jnp.asarray(bins_t[0]))
    first = prepare(here, beside, partner_tables, False)
    across, first = lax.optimization_barrier((across, first))
    across_beside = send(across, lambda q, p, c, g: (q, p, 1 - c, g))
    second = prepare(across, across_beside, partner_tables, False)
    slots = jnp.stack([0, 1 + 2 * core, 2, 3 - 2 * core]).astype(jnp.int32)
    offset_ids = place * owned + slots
    keep = jnp.where(offset_ids < reach[0], jnp.float32(scale), jnp.float32(0.0))
    return stack(own, first, second, jnp.asarray(lag_t), slots, keep)[None]


def solution(mesh):
    placed = (P(None, "fibre", None), P("fibre"), P("fibre"))
    return jax.shard_map(
        per_device,
        mesh=mesh,
        in_specs=placed,
        out_specs=P("fibre", "freq", None, None, None),
        check_vma=False,
    )
```

profile of v0, /device:TPU:21, one launch (start us, length us, event | category | flops | bytes accessed | tf_op | source)
XLA Modules:
  0.0 89.5 jit_solution(14171299491280438572)
XLA Ops:
  0.0 0.7 convert_element_type.3
  0.7 1.4 %broadcast_multiply_fusion.first_ref.second_ref = bf16[2,64,4096]{2,1,0:T(8,128)(2,1)S(1)} fusion(bf16[2,64,4096]{2,1,0:T(8,128)(2,1)} %param.8, bf16[64]{0:T(256)(128)(2,1)S(1)} %convert_element_type.3), kind=kLoop, calls=%fused_computation.3 | loop fusion | flops 524288 | bytes 2097280 | tf_op jit(solution)/shard_map/mul | solution.py:323
  2.0 0.0 copy-start
  2.0 2.1 %collective-permute-start = (bf16[2,64,4096]{2,1,0:T(8,128)(2,1)S(1)}, bf16[2,64,4096]{2,1,0:T(8,128)(2,1)S(1)}, u32[]{:S(2)}, u32[]{:S(2)}) collective-permute-start(bf16[2,64,4096]{2,1,0:T(8,128)(2,1)S(1)} %broadcast_multiply_fusion.first_ref.second_ref), channel_id=1, source_target_pairs={{8,0},{9,1},{10,2},{11,3},{12,4},{13,5},{14,6},{15,7},{16,8},{17,9... | collective-permute-start | bytes 3145736 | tf_op jit(solution)/shard_map/ppermute | solution.py:342
  4.2 0.0 copy-done
  4.2 0.0 copy-start.1
  4.2 12.4 %prepare_own.1.own_ref = bf16[128,128,128]{2,1,0:T(8,128)(2,1)} custom-call(bf16[2,64,4096]{2,1,0:T(8,128)(2,1)} %copy-done, bf16[2,64,4096]{2,1,0:T(8,128)(2,1)} %copy-done, bf16[16,256,256]{2,1,0:T(8,128)(2,1)} %constant.63.clone.fhi_hbm, bf16[16,256,256]{2,1,0:T(8,128)(2,1)} %constant.64.clone.flo_hbm, bf16[16,512,256]{2,1,0:T(8,128)(2,1)} %constant.65.clone.bins_hbm), custom_call_target="tpu_custom_call" | custom-call | flops 2684354560 | bytes 14680064 | tf_op jit(solution)/shard_map/prepare_own/pallas_call | solution.py:229
  16.6 11.4 %collective-permute-done = bf16[2,64,4096]{2,1,0:T(8,128)(2,1)S(1)} collective-permute-done((bf16[2,64,4096]{2,1,0:T(8,128)(2,1)S(1)}, bf16[2,64,4096]{2,1,0:T(8,128)(2,1)S(1)}, u32[]{:S(2)}, u32[]{:S(2)}) %collective-permute-start) | collective-permute-done | bytes 1048608 | tf_op jit(solution)/shard_map/ppermute | solution.py:342
  28.0 0.0 copy-done.1
  28.0 1.2 %broadcast_select_fusion = (bf16[2,64,4096]{2,1,0:T(8,128)(2,1)S(1)}, bf16[2,64,4096]{2,1,0:T(8,128)(2,1)}, bf16[2,64,4096]{2,1,0:T(8,128)(2,1)S(1)}) fusion(bf16[2,64,4096]{2,1,0:T(8,128)(2,1)S(1)} %collective-permute-done, pred[]{:T(512)S(6)} %and.26, pred[]{:T(512)S(6)} %eq.15, pred[]{:T(512)S(6)} %and.24, bf16[2,64,4096]{2,1,0:T(8,128)(2,1)S(1)} %copy-done.1, ...), kind=kLoop, calls=%fused_computation | loop fusion | flops 2097152 | bytes 5243011 | tf_op jit(solution)/shard_map/jit(_where)/select_n | solution.py:347
  29.2 3.4 %collective-permute-start.2 = (bf16[2,64,4096]{2,1,0:T(8,128)(2,1)S(1)}, bf16[2,64,4096]{2,1,0:T(8,128)(2,1)S(1)}, u32[]{:S(2)}, u32[]{:S(2)}) collective-permute-start(bf16[2,64,4096]{2,1,0:T(8,128)(2,1)S(1)} %get-tuple-element.15), channel_id=1, source_target_pairs={{2,0},{3,1},{1,2},{8,3},{6,4},{7,5},{5,6},{12,7},{10,8},{11,9},{9,... | collective-permute-start | bytes 3145736 | tf_op jit(solution)/shard_map/ppermute | solution.py:342
  32.7 3.0 %collective-permute-start.1 = (bf16[2,64,4096]{2,1,0:T(8,128)(2,1)S(1)}, bf16[2,64,4096]{2,1,0:T(8,128)(2,1)S(1)}, u32[]{:S(2)}, u32[]{:S(2)}) collective-permute-start(bf16[2,64,4096]{2,1,0:T(8,128)(2,1)S(1)} %get-tuple-element.17), channel_id=1, source_target_pairs={{4,0},{5,1},{6,2},{7,3},{0,4},{9,5},{2,6},{11,7},{12,8},{13,9},{14... | collective-permute-start | bytes 3145736 | tf_op jit(solution)/shard_map/ppermute | solution.py:342
  35.7 10.5 %collective-permute-done.2.second_ref = bf16[2,64,4096]{2,1,0:T(8,128)(2,1)S(1)} collective-permute-done((bf16[2,64,4096]{2,1,0:T(8,128)(2,1)S(1)}, bf16[2,64,4096]{2,1,0:T(8,128)(2,1)S(1)}, u32[]{:S(2)}, u32[]{:S(2)}) %collective-permute-start.2) | collective-permute-done | bytes 1048608 | tf_op jit(solution)/shard_map/ppermute | solution.py:342
  46.2 0.0 copy-start.4
  46.2 1.1 %copy-done.4 = bf16[2,64,4096]{2,1,0:T(8,128)(2,1)} copy-done((bf16[2,64,4096]{2,1,0:T(8,128)(2,1)}, bf16[2,64,4096]{2,1,0:T(8,128)(2,1)S(1)}, u32[]{:S(2)}) %copy-start.4) | copy-done | bytes 1048600
  47.3 10.4 %prepare_partners.2.first_ref = bf16[128,128,128]{2,1,0:T(8,128)(2,1)} custom-call(bf16[2,64,4096]{2,1,0:T(8,128)(2,1)} %get-tuple-element.16.first_ref, bf16[2,64,4096]{2,1,0:T(8,128)(2,1)} %copy-done.4, bf16[16,256,256]{2,1,0:T(8,128)(2,1)} %constant.63.clone.fhi_hbm, bf16[16,256,256]{2,1,0:T(8,128)(2,1)} %constant.64.clone.flo_hbm, ...), custom_call_target="tpu_custom_call" | custom-call | flops 2684354560 | bytes 14680064 | tf_op jit(solution)/shard_map/prepare_partners/pallas_call | solution.py:229
  57.7 1.6 %collective-permute-done.1.first_ref = bf16[2,64,4096]{2,1,0:T(8,128)(2,1)S(1)} collective-permute-done((bf16[2,64,4096]{2,1,0:T(8,128)(2,1)S(1)}, bf16[2,64,4096]{2,1,0:T(8,128)(2,1)S(1)}, u32[]{:S(2)}, u32[]{:S(2)}) %collective-permute-start.1) | collective-permute-done | bytes 1048608 | tf_op jit(solution)/shard_map/ppermute | solution.py:342
  59.3 0.0 copy-start.2
  59.3 0.8 collective-permute-start.3
  60.8 0.6 compare_select_fusion
  61.4 1.0 %collective-permute-done.3.second_ref = bf16[2,64,4096]{2,1,0:T(8,128)(2,1)S(1)} collective-permute-done((bf16[2,64,4096]{2,1,0:T(8,128)(2,1)S(1)}, bf16[2,64,4096]{2,1,0:T(8,128)(2,1)S(1)}, u32[]{:S(2)}, u32[]{:S(2)}) %collective-permute-start.3) | collective-permute-done | bytes 1048608 | tf_op jit(solution)/shard_map/ppermute | solution.py:342
  62.4 0.0 copy-done.2
  62.4 0.0 copy-start.3
  62.4 1.1 %copy-done.3 = bf16[2,64,4096]{2,1,0:T(8,128)(2,1)} copy-done((bf16[2,64,4096]{2,1,0:T(8,128)(2,1)}, bf16[2,64,4096]{2,1,0:T(8,128)(2,1)S(1)}, u32[]{:S(2)}) %copy-start.3) | copy-done | bytes 1048600
  63.5 10.4 %prepare_partners.3.second_ref = bf16[128,128,128]{2,1,0:T(8,128)(2,1)} custom-call(bf16[2,64,4096]{2,1,0:T(8,128)(2,1)} %copy-done.2, bf16[2,64,4096]{2,1,0:T(8,128)(2,1)} %copy-done.3, bf16[16,256,256]{2,1,0:T(8,128)(2,1)} %constant.63.clone.fhi_hbm, bf16[16,256,256]{2,1,0:T(8,128)(2,1)} %constant.64.clone.flo_hbm, ...), custom_call_target="tpu_custom_call" | custom-call | flops 2684354560 | bytes 14680064 | tf_op jit(solution)/shard_map/prepare_partners/pallas_call | solution.py:229
  73.9 15.5 %stack_lags.1 = f32[4,64,64,128]{3,2,1,0:T(8,128)} custom-call(bf16[128,128,128]{2,1,0:T(8,128)(2,1)} %prepare_own.1.own_ref, bf16[128,128,128]{2,1,0:T(8,128)(2,1)} %prepare_partners.2.first_ref, bf16[128,128,128]{2,1,0:T(8,128)(2,1)} %prepare_partners.3.second_ref, bf16[128,256]{1,0:T(8,128)(2,1)} %constant.67.clone.lag_ref, s32[4]{0:T(128)} %get-tuple-element.14.slot_ref, ...), custom_call_target="tpu_custom_call" | custom-call | tf_op jit(solution)/shard_map/stack_lags/pallas_call | solution.py:292
Async XLA Ops:
  2.0 2.2 %copy-start = (bf16[2,64,4096]{2,1,0:T(8,128)(2,1)}, bf16[2,64,4096]{2,1,0:T(8,128)(2,1)S(1)}, u32[]{:S(2)}) copy-start(bf16[2,64,4096]{2,1,0:T(8,128)(2,1)S(1)} %broadcast_multiply_fusion.first_ref.second_ref) | copy-start | bytes 3145732
  2.0 25.9 %collective-permute-start = (bf16[2,64,4096]{2,1,0:T(8,128)(2,1)S(1)}, bf16[2,64,4096]{2,1,0:T(8,128)(2,1)S(1)}, u32[]{:S(2)}, u32[]{:S(2)}) collective-permute-start(bf16[2,64,4096]{2,1,0:T(8,128)(2,1)S(1)} %broadcast_multiply_fusion.first_ref.second_ref), channel_id=1, source_target_pairs={{8,0},{9,1},{10,2},{11,3},{12,4},{13,5},{14,6},{15,7},{16,8},{17,9... | collective-permute-start | bytes 3145736 | tf_op jit(solution)/shard_map/ppermute | solution.py:342
  4.2 23.8 %copy-start.1 = (bf16[2,64,4096]{2,1,0:T(8,128)(2,1)S(1)}, bf16[2,64,4096]{2,1,0:T(8,128)(2,1)}, u32[]{:S(2)}) copy-start(bf16[2,64,4096]{2,1,0:T(8,128)(2,1)} %param.8) | copy-start | bytes 3145732
  29.2 17.0 %collective-permute-start.2 = (bf16[2,64,4096]{2,1,0:T(8,128)(2,1)S(1)}, bf16[2,64,4096]{2,1,0:T(8,128)(2,1)S(1)}, u32[]{:S(2)}, u32[]{:S(2)}) collective-permute-start(bf16[2,64,4096]{2,1,0:T(8,128)(2,1)S(1)} %get-tuple-element.15), channel_id=1, source_target_pairs={{2,0},{3,1},{1,2},{8,3},{6,4},{7,5},{5,6},{12,7},{10,8},{11,9},{9,... | collective-permute-start | bytes 3145736 | tf_op jit(solution)/shard_map/ppermute | solution.py:342
  32.7 26.7 %collective-permute-start.1 = (bf16[2,64,4096]{2,1,0:T(8,128)(2,1)S(1)}, bf16[2,64,4096]{2,1,0:T(8,128)(2,1)S(1)}, u32[]{:S(2)}, u32[]{:S(2)}) collective-permute-start(bf16[2,64,4096]{2,1,0:T(8,128)(2,1)S(1)} %get-tuple-element.17), channel_id=1, source_target_pairs={{4,0},{5,1},{6,2},{7,3},{0,4},{9,5},{2,6},{11,7},{12,8},{13,9},{14... | collective-permute-start | bytes 3145736 | tf_op jit(solution)/shard_map/ppermute | solution.py:342
  46.2 1.1 %copy-start.4 = (bf16[2,64,4096]{2,1,0:T(8,128)(2,1)}, bf16[2,64,4096]{2,1,0:T(8,128)(2,1)S(1)}, u32[]{:S(2)}) copy-start(bf16[2,64,4096]{2,1,0:T(8,128)(2,1)S(1)} %collective-permute-done.2.second_ref) | copy-start | bytes 3145732
  59.3 3.1 %copy-start.2 = (bf16[2,64,4096]{2,1,0:T(8,128)(2,1)}, bf16[2,64,4096]{2,1,0:T(8,128)(2,1)S(1)}, u32[]{:S(2)}) copy-start(bf16[2,64,4096]{2,1,0:T(8,128)(2,1)S(1)} %collective-permute-done.1.first_ref) | copy-start | bytes 3145732
  59.3 3.1 %collective-permute-start.3 = (bf16[2,64,4096]{2,1,0:T(8,128)(2,1)S(1)}, bf16[2,64,4096]{2,1,0:T(8,128)(2,1)S(1)}, u32[]{:S(2)}, u32[]{:S(2)}) collective-permute-start(bf16[2,64,4096]{2,1,0:T(8,128)(2,1)S(1)} %collective-permute-done.1.first_ref), channel_id=1, source_target_pairs={{2,0},{3,1},{0,2},{1,3},{6,4},{7,5},{4,6},{5,7},{10,8},{11,9},{8,1... | collective-permute-start | bytes 3145736 | tf_op jit(solution)/shard_map/ppermute | solution.py:342
  62.4 1.1 %copy-start.3 = (bf16[2,64,4096]{2,1,0:T(8,128)(2,1)}, bf16[2,64,4096]{2,1,0:T(8,128)(2,1)S(1)}, u32[]{:S(2)}) copy-start(bf16[2,64,4096]{2,1,0:T(8,128)(2,1)S(1)} %collective-permute-done.3.second_ref) | copy-start | bytes 3145732
where the time goes:
time: 90.7 us; the launch traced here: 89.5 us
  Pallas kernels  48.8 us (54%)
  waiting for transfers between devices  24.5 us (27%)
  starting transfers between devices  9.32 us (10%)
  other arithmetic  3.89 us (4%)
  local copies, waits for them, and re-layouts  2.14 us (2%)
    pallas_call x3, Pallas kernels, prepare(): pl.pallas_call(functools.partial(prepare_kernel, own), out_shape=jax.Shap...  33.3 us
    ppermute x4, waiting for transfers between devices, send(): return lax.ppermute(payload, ('fibre', 'freq'), pairs)  24.5 us
    pallas_call x1, Pallas kernels, stack(): pl.pallas_call(functools.partial(stack_kernel, chunks, per_chunk, per_out...  15.5 us
    ppermute x4, starting transfers between devices, send(): return lax.ppermute(payload, ('fibre', 'freq'), pairs)  9.32 us
    unnamed x10, local copies, waits for them, and re-layouts  2.14 us
  transfers between devices with their start and end apart: 4, of which 4 were waited for; matrix products, arithmetic and copies ran while one was open for 1% of the time, Pallas kernels for 25%

commit v1 on v0

--- a/solution.py
+++ b/solution.py
@@ -13,7 +13,7 @@
 BAND = 64
 OFF = 8
 LAGS = 128
-VMEM_LIMIT = 56 * 1024 * 1024
+VMEM_LIMIT = 36 * 1024 * 1024
 
 
 def leak_spectrum(freqs, samples, window, shift, slots, period):
@@ -126,9 +126,10 @@
     return out
 
 
-def prepare_kernel(own, first_ref, second_ref, fhi_hbm, flo_hbm, bins_hbm, out_ref,
-                   fhi, flo, bins, yhi, ylo, spec, wide, sems):
-    windows, channels, samples = first_ref.shape
+def prepare_kernel(own, windows, *refs):
+    records, refs = refs[:-12], refs[-12:]
+    fhi_hbm, flo_hbm, bins_hbm, out_ref, fhi, flo, bins, yhi, ylo, spec, wide, sems = refs
+    channels, samples = records[0].shape
     width = LAGS
     residues = samples // width
     groups = residues // 2
@@ -143,18 +144,15 @@
         copy.start()
 
     step = 16
-    per_window = channels // step
 
     def split(value):
         high = value.astype(jnp.bfloat16)
         return high, (value - high.astype(jnp.float32)).astype(jnp.bfloat16)
 
     def transform(n, carry):
-        w, c = n // per_window, n % per_window
-        for which, ref in enumerate((first_ref, second_ref)):
-            if own and which:
-                continue
-            block = ref[w, pl.ds(pl.multiple_of(c * step, step), step), :].astype(jnp.float32)
+        for index, ref in enumerate(records):
+            which, w = divmod(index, windows)
+            block = ref[pl.ds(pl.multiple_of(n * step, step), step), :].astype(jnp.float32)
             terms = real_dft([block[:, a * width:(a + 1) * width] for a in range(residues)])
             for g in range(groups):
                 if g == 0:
@@ -164,12 +162,12 @@
                 for side, part in enumerate(parts):
                     hi, lo = split(part)
                     for copy_to in ((0, 1) if own else (which,)):
-                        row = pl.multiple_of(w * lanes + copy_to * channels + c * step, step)
+                        row = pl.multiple_of(w * lanes + copy_to * channels + n * step, step)
                         yhi[g, pl.ds(row, step), side * width:(side + 1) * width] = hi
                         ylo[g, pl.ds(row, step), side * width:(side + 1) * width] = lo
         return carry
 
-    lax.fori_loop(0, windows * per_window, transform, 0)
+    lax.fori_loop(0, channels // step, transform, 0)
     copies[0].wait()
     copies[1].wait()
     nt = (((1,), (1,)), ((), ()))
@@ -214,8 +212,8 @@
     lax.fori_loop(0, width, narrow, 0, unroll=8)
 
 
-def prepare(first, second, tables, own):
-    windows, channels, samples = first.shape
+def prepare(records, windows, tables, own):
+    channels, samples = records[0].shape
     forward_hi, forward_lo, bins_t = tables
     width = LAGS
     groups = samples // width // 2
@@ -227,9 +225,9 @@
     vmem_spec = pl.BlockSpec(memory_space=pltpu.VMEM)
     flops = 2 * groups * rows * (3 * 4 * width * width + 8 * width * width)
     return pl.pallas_call(
-        functools.partial(prepare_kernel, own),
+        functools.partial(prepare_kernel, own, windows),
         out_shape=jax.ShapeDtypeStruct(shape, jnp.bfloat16),
-        in_specs=[vmem_spec, vmem_spec, any_spec, any_spec, any_spec],
+        in_specs=[vmem_spec] * len(records) + [any_spec] * 3,
         out_specs=vmem_spec,
         scratch_shapes=[
             pltpu.VMEM(forward_hi.shape, jnp.bfloat16),
@@ -244,7 +242,7 @@
         compiler_params=pltpu.CompilerParams(vmem_limit_bytes=VMEM_LIMIT),
         cost_estimate=pl.CostEstimate(flops=flops, bytes_accessed=14 * 2**20, transcendentals=0),
         name="prepare_own" if own else "prepare_partners",
-    )(first, second, forward_hi, forward_lo, bins_t)
+    )(*records, forward_hi, forward_lo, bins_t)
 
 
 def stack_kernel(chunks, per_chunk, per_out, own_ref, first_ref, second_ref, lag_ref, slot_ref, keep_ref, out_ref, *cross):
@@ -320,7 +318,8 @@
     place = lax.axis_index("freq")
     forward_hi, forward_lo, bins_t, lag_t, scale = build_tables(samples)
     forward_hi, forward_lo = jnp.asarray(forward_hi), jnp.asarray(forward_lo)
-    masked = traces * live.astype(traces.dtype)[None, :, None]
+    alive = live.astype(traces.dtype)[:, None]
+    masked = [traces[w] * alive for w in range(windows)]
 
     quads = blocks // owned
     half = owned // 2
@@ -341,19 +340,23 @@
                             pairs.append((rank(*source), rank(q, p, c, g)))
         return lax.ppermute(payload, ("fibre", "freq"), pairs)
 
-    upper = send(masked, lambda q, p, c, g: (q + 1, p, c, g))
-    own = prepare(masked, masked, (forward_hi, forward_lo, jnp.asarray(bins_t[1])), True)
-    upper, own = lax.optimization_barrier((upper, own))
-    core_payload = jnp.where((core == 1) & (place == 0), masked, upper)
-    across_payload = jnp.where((pair == 1) & (place == 0), masked, upper)
-    beside = send(core_payload, lambda q, p, c, g: (q + c * g, p, 1 - c, 1 - g if c else g))
-    across = send(across_payload, lambda q, p, c, g: (q + p * g, 1 - p, c, g))
-    here = jnp.where(place == 0, masked, upper)
+    def from_neighbours(mine, upper):
+        core_payload = jnp.where((core == 1) & (place == 0), mine, upper)
+        across_payload = jnp.where((pair == 1) & (place == 0), mine, upper)
+        beside = send(core_payload, lambda q, p, c, g: (q + c * g, p, 1 - c, 1 - g if c else g))
+        across = send(across_payload, lambda q, p, c, g: (q + p * g, 1 - p, c, g))
+        return jnp.where(place == 0, mine, upper), beside, across
+
+    upper = [send(mine, lambda q, p, c, g: (q + 1, p, c, g)) for mine in masked]
+    own = prepare(masked, windows, (forward_hi, forward_lo, jnp.asarray(bins_t[1])), True)
+    upper[0], own = lax.optimization_barrier((upper[0], own))
+    here, beside, across = map(list, zip(*(from_neighbours(mine, up) for mine, up in zip(masked, upper))))
     partner_tables = (forward_hi, forward_lo, jnp.asarray(bins_t[0]))
-    first = prepare(here, beside, partner_tables, False)
-    across, first = lax.optimization_barrier((across, first))
-    across_beside = send(across, lambda q, p, c, g: (q, p, 1 - c, g))
-    second = prepare(across, across_beside, partner_tables, False)
+    across[0], beside[-1] = lax.optimization_barrier((across[0], beside[-1]))
+    first = prepare(here + beside, windows, partner_tables, False)
+    across[-1], first = lax.optimization_barrier((across[-1], first))
+    across_beside = [send(block, lambda q, p, c, g: (q, p, 1 - c, g)) for block in across]
+    second = prepare(across + across_beside, windows, partner_tables, False)
     slots = jnp.stack([0, 1 + 2 * core, 2, 3 - 2 * core]).astype(jnp.int32)
     offset_ids = place * owned + slots
     keep = jnp.where(offset_ids < reach[0], jnp.float32(scale), jnp.float32(0.0))

time: 90.7 us -> 87.8 us (0.968)
  waiting for transfers between devices: 24.5 us -> 9.22 us
  Pallas kernels: 48.8 us -> 37.1 us
  starting transfers between devices: 9.32 us -> 20.9 us
  local copies, waits for them, and re-layouts: 2.14 us -> 13.3 us
  other arithmetic: 3.89 us -> 4.92 us
    ppermute x4 -> x8, waiting for transfers between devices: 24.5 us -> 9.22 us  [send(): return lax.ppermute(payload, ('fibre', 'freq'), pairs)]
    ppermute x4 -> x8, starting transfers between devices: 9.32 us -> 20.9 us  [send(): return lax.ppermute(payload, ('fibre', 'freq'), pairs)]
    unnamed x10 -> x24, local copies, waits for them, and re-layouts: 2.14 us -> 13.3 us
    pallas_call x3, Pallas kernels: 33.3 us -> 24.1 us  [prepare(): pl.pallas_call(functools.partial(prepare_kernel, own, windows), out_shape...]
    pallas_call x1, Pallas kernels: 15.5 us -> 13.1 us  [stack(): pl.pallas_call(functools.partial(stack_kernel, chunks, per_chunk, per_out...]
    select_n x1 -> x2, other arithmetic: 1.24 us -> 2.85 us  [the longest x1 1.7 us: from_neighbours(): core_payload = jnp.where((core == 1) & (place == 0), mine, upper)]
  transfers between devices with their start and end apart: 4 -> 8, of which waited for: 4 -> 3; matrix products, arithmetic and copies ran while one was open for 1% -> 3% of each run, Pallas kernels for 25% -> 18%
where the time goes in v1:
time: 87.8 us; the launch traced here: 86.3 us
  Pallas kernels  37.1 us (42%)
  starting transfers between devices  20.9 us (24%)
  local copies, waits for them, and re-layouts  13.3 us (15%)
  waiting for transfers between devices  9.22 us (11%)
  other arithmetic  4.92 us (6%)
  between operations  0.88 us (1%)
    pallas_call x3, Pallas kernels, prepare(): pl.pallas_call(functools.partial(prepare_kernel, own, windows), out_shape...  24.1 us
    ppermute x8, starting transfers between devices, send(): return lax.ppermute(payload, ('fibre', 'freq'), pairs)  20.9 us
    unnamed x24, local copies, waits for them, and re-layouts  13.3 us
    pallas_call x1, Pallas kernels, stack(): pl.pallas_call(functools.partial(stack_kernel, chunks, per_chunk, per_out...  13.1 us
    ppermute x8, waiting for transfers between devices, send(): return lax.ppermute(payload, ('fibre', 'freq'), pairs)  9.22 us
  transfers between devices with their start and end apart: 8, of which 3 were waited for; matrix products, arithmetic and copies ran while one was open for 3% of the time, Pallas kernels for 18%

profile of v1, /device:TPU:21, one launch (start us, length us, event | category | flops | bytes accessed | tf_op | source)
XLA Modules:
  0.0 86.3 jit_solution(3189509154413644457)
XLA Ops:
  0.0 0.7 convert_element_type.3
  0.7 1.3 %bitcast_multiply_fusion = (bf16[64,4096]{1,0:T(8,128)(2,1)S(1)}, bf16[64,4096]{1,0:T(8,128)(2,1)S(1)}) fusion(bf16[2,64,4096]{2,1,0:T(8,128)(2,1)} %param.8, bf16[64]{0:T(256)(128)(2,1)S(1)} %convert_element_type.3), kind=kLoop, calls=%fused_computation | loop fusion | flops 524288 | bytes 2097280 | tf_op jit(solution)/shard_map/mul | solution.py:322
  2.0 2.1 %collective-permute-start.1 = (bf16[64,4096]{1,0:T(8,128)(2,1)S(1)}, bf16[64,4096]{1,0:T(8,128)(2,1)}, u32[]{:S(2)}, u32[]{:S(2)}) collective-permute-start(bf16[64,4096]{1,0:T(8,128)(2,1)S(1)} %get-tuple-element.19.refs_1_), channel_id=1, source_target_pairs={{8,0},{9,1},{10,2},{11,3},{12,4},{13,5},{14,6},{15,7},{16,8},{17,9... | collective-permute-start | bytes 1572872 | tf_op jit(solution)/shard_map/ppermute | solution.py:341
  4.1 2.1 %collective-permute-start = (bf16[64,4096]{1,0:T(8,128)(2,1)S(1)}, bf16[64,4096]{1,0:T(8,128)(2,1)}, u32[]{:S(2)}, u32[]{:S(2)}) collective-permute-start(bf16[64,4096]{1,0:T(8,128)(2,1)S(1)} %get-tuple-element.20.refs_0_), channel_id=1, source_target_pairs={{8,0},{9,1},{10,2},{11,3},{12,4},{13,5},{14,6},{15,7},{16,8},{17,9... | collective-permute-start | bytes 1572872 | tf_op jit(solution)/shard_map/ppermute | solution.py:341
  6.2 0.0 copy-start
  6.2 1.6 %copy-done = bf16[16,256,256]{2,1,0:T(8,128)(2,1)S(1)} copy-done((bf16[16,256,256]{2,1,0:T(8,128)(2,1)S(1)}, bf16[16,256,256]{2,1,0:T(8,128)(2,1)}, u32[]{:S(2)}) %copy-start) | copy-done | bytes 2097176
  7.8 0.0 copy-start.2
  7.8 1.6 %copy-done.2 = bf16[16,256,256]{2,1,0:T(8,128)(2,1)S(1)} copy-done((bf16[16,256,256]{2,1,0:T(8,128)(2,1)S(1)}, bf16[16,256,256]{2,1,0:T(8,128)(2,1)}, u32[]{:S(2)}) %copy-start.2) | copy-done | bytes 2097176
  9.4 0.0 copy-start.10
  9.4 2.2 %copy-done.10 = bf16[16,512,256]{2,1,0:T(8,128)(2,1)S(1)} copy-done((bf16[16,512,256]{2,1,0:T(8,128)(2,1)S(1)}, bf16[16,512,256]{2,1,0:T(8,128)(2,1)}, u32[]{:S(2)}) %copy-start.10) | copy-done | bytes 4194328
  11.6 0.0 copy-start.4
  11.6 8.3 %prepare_own.1.own_ref = bf16[128,128,128]{2,1,0:T(8,128)(2,1)S(1)} custom-call(bf16[64,4096]{1,0:T(8,128)(2,1)S(1)} %get-tuple-element.20.refs_0_, bf16[64,4096]{1,0:T(8,128)(2,1)S(1)} %get-tuple-element.19.refs_1_, bf16[16,256,256]{2,1,0:T(8,128)(2,1)S(1)} %copy-done.2, bf16[16,256,256]{2,1,0:T(8,128)(2,1)S(1)} %copy-done, bf16[16,512,256]{2,1,0:T(8,128)(2,1)S(1)} %copy-done.10), custom_call_target="tpu_custom_call" | custom-call | flops 2684354560 | bytes 14680064 | tf_op jit(solution)/shard_map/prepare_own/pallas_call | solution.py:227
  19.9 0.0 copy-start.8
  19.9 0.0 copy-start.1
  19.9 0.0 collective-permute-done.1
  20.0 1.7 %broadcast_select_fusion = (bf16[64,4096]{1,0:T(8,128)(2,1)S(1)}, bf16[64,4096]{1,0:T(8,128)(2,1)S(1)}, bf16[64,4096]{1,0:T(8,128)(2,1)S(1)}) fusion(bf16[64,4096]{1,0:T(8,128)(2,1)S(1)} %get-tuple-element.19.refs_1_, bf16[64,4096]{1,0:T(8,128)(2,1)} %collective-permute-done.1, pred[]{:T(512)S(6)} %and.28, pred[]{:T(512)S(6)} %eq.10, pred[]{:T(512)S(6)} %and.26), kind=kLoop, calls=%fused_computation.2 | loop fusion | flops 786432 | bytes 2621443 | tf_op jit(solution)/shard_map/jit(_where)/select_n | solution.py:344
  21.7 3.3 %collective-permute-start.5 = (bf16[64,4096]{1,0:T(8,128)(2,1)S(1)}, bf16[64,4096]{1,0:T(8,128)(2,1)S(1)}, u32[]{:S(2)}, u32[]{:S(2)}) collective-permute-start(bf16[64,4096]{1,0:T(8,128)(2,1)S(1)} %get-tuple-element.21), channel_id=1, source_target_pairs={{2,0},{3,1},{1,2},{8,3},{6,4},{7,5},{5,6},{12,7},{10,8},{11,9},{9,... | collective-permute-start | bytes 1572872 | tf_op jit(solution)/shard_map/ppermute | solution.py:341
  24.9 3.1 %collective-permute-done = bf16[64,4096]{1,0:T(8,128)(2,1)} collective-permute-done((bf16[64,4096]{1,0:T(8,128)(2,1)S(1)}, bf16[64,4096]{1,0:T(8,128)(2,1)}, u32[]{:S(2)}, u32[]{:S(2)}) %collective-permute-start) | collective-permute-done | bytes 524320 | tf_op jit(solution)/shard_map/ppermute | solution.py:341
  28.0 1.1 %broadcast_select_fusion.4 = (bf16[64,4096]{1,0:T(8,128)(2,1)S(1)}, bf16[64,4096]{1,0:T(8,128)(2,1)S(1)}, bf16[64,4096]{1,0:T(8,128)(2,1)S(1)}) fusion(bf16[64,4096]{1,0:T(8,128)(2,1)S(1)} %get-tuple-element.20.refs_0_, bf16[64,4096]{1,0:T(8,128)(2,1)} %collective-permute-done, pred[]{:T(512)S(6)} %and.26, pred[]{:T(512)S(6)} %and.28, pred[]{:T(512)S(6)} %eq.10), kind=kLoop, calls=%fused_computation.6 | loop fusion | flops 786432 | bytes 2621443 | tf_op jit(solution)/shard_map/jit(_where)/select_n | solution.py:345
  29.2 3.0 %collective-permute-start.4 = (bf16[64,4096]{1,0:T(8,128)(2,1)S(1)}, bf16[64,4096]{1,0:T(8,128)(2,1)S(1)}, u32[]{:S(2)}, u32[]{:S(2)}) collective-permute-start(bf16[64,4096]{1,0:T(8,128)(2,1)S(1)} %get-tuple-element.24), channel_id=1, source_target_pairs={{4,0},{5,1},{6,2},{7,3},{0,4},{9,5},{2,6},{11,7},{12,8},{13,9},{14... | collective-permute-start | bytes 1572872 | tf_op jit(solution)/shard_map/ppermute | solution.py:341
  32.2 3.7 %collective-permute-start.3 = (bf16[64,4096]{1,0:T(8,128)(2,1)S(1)}, bf16[64,4096]{1,0:T(8,128)(2,1)S(1)}, u32[]{:S(2)}, u32[]{:S(2)}) collective-permute-start(bf16[64,4096]{1,0:T(8,128)(2,1)S(1)} %get-tuple-element.25), channel_id=1, source_target_pairs={{2,0},{3,1},{1,2},{8,3},{6,4},{7,5},{5,6},{12,7},{10,8},{11,9},{9,... | collective-permute-start | bytes 1572872 | tf_op jit(solution)/shard_map/ppermute | solution.py:341
  35.9 2.2 %collective-permute-start.2 = (bf16[64,4096]{1,0:T(8,128)(2,1)S(1)}, bf16[64,4096]{1,0:T(8,128)(2,1)S(1)}, u32[]{:S(2)}, u32[]{:S(2)}) collective-permute-start(bf16[64,4096]{1,0:T(8,128)(2,1)S(1)} %get-tuple-element.23), channel_id=1, source_target_pairs={{4,0},{5,1},{6,2},{7,3},{0,4},{9,5},{2,6},{11,7},{12,8},{13,9},{14... | collective-permute-start | bytes 1572872 | tf_op jit(solution)/shard_map/ppermute | solution.py:341
  38.1 0.0 collective-permute-done.5.refs_3_
  38.1 4.8 %collective-permute-done.4.refs_0_ = bf16[64,4096]{1,0:T(8,128)(2,1)S(1)} collective-permute-done((bf16[64,4096]{1,0:T(8,128)(2,1)S(1)}, bf16[64,4096]{1,0:T(8,128)(2,1)S(1)}, u32[]{:S(2)}, u32[]{:S(2)}) %collective-permute-start.4) | collective-permute-done | bytes 524320 | tf_op jit(solution)/shard_map/ppermute | solution.py:341
  42.9 4.5 %collective-permute-start.6 = (bf16[64,4096]{1,0:T(8,128)(2,1)S(1)}, bf16[64,4096]{1,0:T(8,128)(2,1)}, u32[]{:S(2)}, u32[]{:S(2)}) collective-permute-start(bf16[64,4096]{1,0:T(8,128)(2,1)S(1)} %collective-permute-done.4.refs_0_), channel_id=1, source_target_pairs={{2,0},{3,1},{0,2},{1,3},{6,4},{7,5},{4,6},{5,7},{10,8},{11,9},{8,1... | collective-permute-start | bytes 1572872 | tf_op jit(solution)/shard_map/ppermute | solution.py:341
  47.5 0.0 collective-permute-done.3.refs_2_
  47.5 0.0 copy-done.4
  47.5 0.0 copy-done.1
  47.5 7.2 %prepare_partners.2.first_ref = bf16[128,128,128]{2,1,0:T(8,128)(2,1)S(1)} custom-call(bf16[64,4096]{1,0:T(8,128)(2,1)S(1)} %get-tuple-element.26.refs_0_, bf16[64,4096]{1,0:T(8,128)(2,1)S(1)} %get-tuple-element.22.refs_1_, bf16[64,4096]{1,0:T(8,128)(2,1)S(1)} %collective-permute-done.3.refs_2_, bf16[64,4096]{1,0:T(8,128)(2,1)S(1)} %collective-permute-done.5.refs_3_, ...), custom_call_target="tpu_custom_call" | custom-call | flops 2684354560 | bytes 14680064 | tf_op jit(solution)/shard_map/prepare_partners/pallas_call | solution.py:227
  54.7 0.0 copy-done.8
  54.7 0.0 copy-start.6
  54.7 1.9 %copy-done.6 = bf16[128,128,128]{2,1,0:T(8,128)(2,1)} copy-done((bf16[128,128,128]{2,1,0:T(8,128)(2,1)}, bf16[128,128,128]{2,1,0:T(8,128)(2,1)S(1)}, u32[]{:S(2)}) %copy-start.6) | copy-done | bytes 4194328
  56.7 0.0 collective-permute-done.2.refs_1_
  56.7 0.0 collective-permute-start.7
  57.3 0.1 compare_select_fusion
  57.4 0.0 collective-permute-done.6.refs_2_
  57.4 1.3 %collective-permute-done.7.refs_3_ = bf16[64,4096]{1,0:T(8,128)(2,1)} collective-permute-done((bf16[64,4096]{1,0:T(8,128)(2,1)S(1)}, bf16[64,4096]{1,0:T(8,128)(2,1)}, u32[]{:S(2)}, u32[]{:S(2)}) %collective-permute-start.7) | collective-permute-done | bytes 524320 | tf_op jit(solution)/shard_map/ppermute | solution.py:341
  58.7 0.0 copy-start.3
  58.7 1.6 %copy-done.3 = bf16[16,256,256]{2,1,0:T(8,128)(2,1)S(1)} copy-done((bf16[16,256,256]{2,1,0:T(8,128)(2,1)S(1)}, bf16[16,256,256]{2,1,0:T(8,128)(2,1)}, u32[]{:S(2)}) %copy-start.3) | copy-done | bytes 2097176
  60.3 0.0 copy-start.5
  60.3 2.2 %copy-done.5 = bf16[16,512,256]{2,1,0:T(8,128)(2,1)S(1)} copy-done((bf16[16,512,256]{2,1,0:T(8,128)(2,1)S(1)}, bf16[16,512,256]{2,1,0:T(8,128)(2,1)}, u32[]{:S(2)}) %copy-start.5) | copy-done | bytes 4194328
  62.5 0.0 copy-start.11
  62.5 8.6 %prepare_partners.3.second_ref = bf16[128,128,128]{2,1,0:T(8,128)(2,1)S(1)} custom-call(bf16[64,4096]{1,0:T(8,128)(2,1)S(1)} %collective-permute-done.4.refs_0_, bf16[64,4096]{1,0:T(8,128)(2,1)S(1)} %collective-permute-done.2.refs_1_, bf16[64,4096]{1,0:T(8,128)(2,1)} %collective-permute-done.6.refs_2_, bf16[64,4096]{1,0:T(8,128)(2,1)} %collective-permute-done.7.refs_3_, ...), custom_call_target="tpu_custom_call" | custom-call | flops 2684354560 | bytes 14680064 | tf_op jit(solution)/shard_map/prepare_partners/pallas_call | solution.py:227
  71.1 0.0 copy-done.7
  71.1 0.0 copy-done.11
  71.1 0.0 copy-start.9
  71.1 2.2 %copy-done.9 = bf16[128,128,128]{2,1,0:T(8,128)(2,1)S(1)} copy-done((bf16[128,128,128]{2,1,0:T(8,128)(2,1)S(1)}, bf16[128,128,128]{2,1,0:T(8,128)(2,1)}, u32[]{:S(2)}) %copy-start.9) | copy-done | bytes 4194328
  73.3 13.1 %stack_lags.1 = f32[4,64,64,128]{3,2,1,0:T(8,128)} custom-call(bf16[128,128,128]{2,1,0:T(8,128)(2,1)S(1)} %copy-done.9, bf16[128,128,128]{2,1,0:T(8,128)(2,1)S(1)} %copy-done.7, bf16[128,128,128]{2,1,0:T(8,128)(2,1)S(1)} %prepare_partners.3.second_ref, bf16[128,256]{1,0:T(8,128)(2,1)S(1)} %copy-done.11, s32[4]{0:T(128)S(1)} %get-tuple-element.18.slot_ref, ...), custom_call_target="tpu_custom_call" | custom-call | tf_op jit(solution)/shard_map/stack_lags/pallas_call | solution.py:290
  (1 shorter events, 0.0 us)
Async XLA Ops:
  2.0 17.9 %collective-permute-start.1 = (bf16[64,4096]{1,0:T(8,128)(2,1)S(1)}, bf16[64,4096]{1,0:T(8,128)(2,1)}, u32[]{:S(2)}, u32[]{:S(2)}) collective-permute-start(bf16[64,4096]{1,0:T(8,128)(2,1)S(1)} %get-tuple-element.19.refs_1_), channel_id=1, source_target_pairs={{8,0},{9,1},{10,2},{11,3},{12,4},{13,5},{14,6},{15,7},{16,8},{17,9... | collective-permute-start | bytes 1572872 | tf_op jit(solution)/shard_map/ppermute | solution.py:341
  4.1 23.9 %collective-permute-start = (bf16[64,4096]{1,0:T(8,128)(2,1)S(1)}, bf16[64,4096]{1,0:T(8,128)(2,1)}, u32[]{:S(2)}, u32[]{:S(2)}) collective-permute-start(bf16[64,4096]{1,0:T(8,128)(2,1)S(1)} %get-tuple-element.20.refs_0_), channel_id=1, source_target_pairs={{8,0},{9,1},{10,2},{11,3},{12,4},{13,5},{14,6},{15,7},{16,8},{17,9... | collective-permute-start | bytes 1572872 | tf_op jit(solution)/shard_map/ppermute | solution.py:341
  6.2 1.6 %copy-start = (bf16[16,256,256]{2,1,0:T(8,128)(2,1)S(1)}, bf16[16,256,256]{2,1,0:T(8,128)(2,1)}, u32[]{:S(2)}) copy-start(bf16[16,256,256]{2,1,0:T(8,128)(2,1)} %constant.64.clone.refs_3_.refs_5_) | copy-start | bytes 6291460
  7.8 1.6 %copy-start.2 = (bf16[16,256,256]{2,1,0:T(8,128)(2,1)S(1)}, bf16[16,256,256]{2,1,0:T(8,128)(2,1)}, u32[]{:S(2)}) copy-start(bf16[16,256,256]{2,1,0:T(8,128)(2,1)} %constant.63.clone.refs_2_.refs_4_) | copy-start | bytes 6291460
  9.4 2.2 %copy-start.10 = (bf16[16,512,256]{2,1,0:T(8,128)(2,1)S(1)}, bf16[16,512,256]{2,1,0:T(8,128)(2,1)}, u32[]{:S(2)}) copy-start(bf16[16,512,256]{2,1,0:T(8,128)(2,1)} %constant.65.clone.refs_4_) | copy-start | bytes 12582916
  11.6 35.9 %copy-start.4 = (bf16[16,512,256]{2,1,0:T(8,128)(2,1)S(1)}, bf16[16,512,256]{2,1,0:T(8,128)(2,1)}, u32[]{:S(2)}) copy-start(bf16[16,512,256]{2,1,0:T(8,128)(2,1)} %constant.66.clone.refs_6_) | copy-start | bytes 12582916
  19.9 34.8 %copy-start.8 = (bf16[128,128,128]{2,1,0:T(8,128)(2,1)}, bf16[128,128,128]{2,1,0:T(8,128)(2,1)S(1)}, u32[]{:S(2)}) copy-start(bf16[128,128,128]{2,1,0:T(8,128)(2,1)S(1)} %prepare_own.1.own_ref) | copy-start | bytes 12582916
  19.9 27.6 %copy-start.1 = (bf16[16,256,256]{2,1,0:T(8,128)(2,1)S(1)}, bf16[16,256,256]{2,1,0:T(8,128)(2,1)}, u32[]{:S(2)}) copy-start(bf16[16,256,256]{2,1,0:T(8,128)(2,1)} %constant.64.clone.refs_3_.refs_5_) | copy-start | bytes 6291460
  21.7 16.4 %collective-permute-start.5 = (bf16[64,4096]{1,0:T(8,128)(2,1)S(1)}, bf16[64,4096]{1,0:T(8,128)(2,1)S(1)}, u32[]{:S(2)}, u32[]{:S(2)}) collective-permute-start(bf16[64,4096]{1,0:T(8,128)(2,1)S(1)} %get-tuple-element.21), channel_id=1, source_target_pairs={{2,0},{3,1},{1,2},{8,3},{6,4},{7,5},{5,6},{12,7},{10,8},{11,9},{9,... | collective-permute-start | bytes 1572872 | tf_op jit(solution)/shard_map/ppermute | solution.py:341
  29.2 13.8 %collective-permute-start.4 = (bf16[64,4096]{1,0:T(8,128)(2,1)S(1)}, bf16[64,4096]{1,0:T(8,128)(2,1)S(1)}, u32[]{:S(2)}, u32[]{:S(2)}) collective-permute-start(bf16[64,4096]{1,0:T(8,128)(2,1)S(1)} %get-tuple-element.24), channel_id=1, source_target_pairs={{4,0},{5,1},{6,2},{7,3},{0,4},{9,5},{2,6},{11,7},{12,8},{13,9},{14... | collective-permute-start | bytes 1572872 | tf_op jit(solution)/shard_map/ppermute | solution.py:341
  32.2 15.3 %collective-permute-start.3 = (bf16[64,4096]{1,0:T(8,128)(2,1)S(1)}, bf16[64,4096]{1,0:T(8,128)(2,1)S(1)}, u32[]{:S(2)}, u32[]{:S(2)}) collective-permute-start(bf16[64,4096]{1,0:T(8,128)(2,1)S(1)} %get-tuple-element.25), channel_id=1, source_target_pairs={{2,0},{3,1},{1,2},{8,3},{6,4},{7,5},{5,6},{12,7},{10,8},{11,9},{9,... | collective-permute-start | bytes 1572872 | tf_op jit(solution)/shard_map/ppermute | solution.py:341
  35.9 20.7 %collective-permute-start.2 = (bf16[64,4096]{1,0:T(8,128)(2,1)S(1)}, bf16[64,4096]{1,0:T(8,128)(2,1)S(1)}, u32[]{:S(2)}, u32[]{:S(2)}) collective-permute-start(bf16[64,4096]{1,0:T(8,128)(2,1)S(1)} %get-tuple-element.23), channel_id=1, source_target_pairs={{4,0},{5,1},{6,2},{7,3},{0,4},{9,5},{2,6},{11,7},{12,8},{13,9},{14... | collective-permute-start | bytes 1572872 | tf_op jit(solution)/shard_map/ppermute | solution.py:341
  42.9 14.5 %collective-permute-start.6 = (bf16[64,4096]{1,0:T(8,128)(2,1)S(1)}, bf16[64,4096]{1,0:T(8,128)(2,1)}, u32[]{:S(2)}, u32[]{:S(2)}) collective-permute-start(bf16[64,4096]{1,0:T(8,128)(2,1)S(1)} %collective-permute-done.4.refs_0_), channel_id=1, source_target_pairs={{2,0},{3,1},{0,2},{1,3},{6,4},{7,5},{4,6},{5,7},{10,8},{11,9},{8,1... | collective-permute-start | bytes 1572872 | tf_op jit(solution)/shard_map/ppermute | solution.py:341
  54.7 1.9 %copy-start.6 = (bf16[128,128,128]{2,1,0:T(8,128)(2,1)}, bf16[128,128,128]{2,1,0:T(8,128)(2,1)S(1)}, u32[]{:S(2)}) copy-start(bf16[128,128,128]{2,1,0:T(8,128)(2,1)S(1)} %prepare_partners.2.first_ref) | copy-start | bytes 12582916
  56.7 2.0 %collective-permute-start.7 = (bf16[64,4096]{1,0:T(8,128)(2,1)S(1)}, bf16[64,4096]{1,0:T(8,128)(2,1)}, u32[]{:S(2)}, u32[]{:S(2)}) collective-permute-start(bf16[64,4096]{1,0:T(8,128)(2,1)S(1)} %collective-permute-done.2.refs_1_), channel_id=1, source_target_pairs={{2,0},{3,1},{0,2},{1,3},{6,4},{7,5},{4,6},{5,7},{10,8},{11,9},{8,1... | collective-permute-start | bytes 1572872 | tf_op jit(solution)/shard_map/ppermute | solution.py:341
  58.7 1.6 %copy-start.3 = (bf16[16,256,256]{2,1,0:T(8,128)(2,1)S(1)}, bf16[16,256,256]{2,1,0:T(8,128)(2,1)}, u32[]{:S(2)}) copy-start(bf16[16,256,256]{2,1,0:T(8,128)(2,1)} %constant.63.clone.refs_2_.refs_4_) | copy-start | bytes 6291460
  60.3 2.2 %copy-start.5 = (bf16[16,512,256]{2,1,0:T(8,128)(2,1)S(1)}, bf16[16,512,256]{2,1,0:T(8,128)(2,1)}, u32[]{:S(2)}) copy-start(bf16[16,512,256]{2,1,0:T(8,128)(2,1)} %constant.66.clone.refs_6_) | copy-start | bytes 12582916
  62.5 8.6 %copy-start.7 = (bf16[128,128,128]{2,1,0:T(8,128)(2,1)S(1)}, bf16[128,128,128]{2,1,0:T(8,128)(2,1)}, u32[]{:S(2)}) copy-start(bf16[128,128,128]{2,1,0:T(8,128)(2,1)} %copy-done.6) | copy-start | bytes 12582916
  62.5 8.6 %copy-start.11 = (bf16[128,256]{1,0:T(8,128)(2,1)S(1)}, bf16[128,256]{1,0:T(8,128)(2,1)}, u32[]{:S(2)}) copy-start(bf16[128,256]{1,0:T(8,128)(2,1)} %constant.67.clone.lag_ref) | copy-start | bytes 196612
  71.1 2.2 %copy-start.9 = (bf16[128,128,128]{2,1,0:T(8,128)(2,1)S(1)}, bf16[128,128,128]{2,1,0:T(8,128)(2,1)}, u32[]{:S(2)}) copy-start(bf16[128,128,128]{2,1,0:T(8,128)(2,1)} %copy-done.8) | copy-start | bytes 12582916

commit v2 on v1

--- a/solution.py
+++ b/solution.py
@@ -13,7 +13,7 @@
 BAND = 64
 OFF = 8
 LAGS = 128
-VMEM_LIMIT = 36 * 1024 * 1024
+VMEM_LIMIT = 50 * 2**20
 
 
 def leak_spectrum(freqs, samples, window, shift, slots, period):
@@ -126,23 +126,14 @@
     return out
 
 
-def prepare_kernel(own, windows, *refs):
-    records, refs = refs[:-12], refs[-12:]
-    fhi_hbm, flo_hbm, bins_hbm, out_ref, fhi, flo, bins, yhi, ylo, spec, wide, sems = refs
+def whiten_into_bins(own, windows, records, copies, fhi, flo, bins, yhi, ylo, spec, wide):
     channels, samples = records[0].shape
     width = LAGS
     residues = samples // width
     groups = residues // 2
     rows = 2 * windows * channels
     lanes = 2 * channels
-    depth = windows * groups * 4
-    copies = [
-        pltpu.make_async_copy(src, dst, sems.at[i])
-        for i, (src, dst) in enumerate(((fhi_hbm, fhi), (flo_hbm, flo), (bins_hbm, bins)))
-    ]
-    for copy in copies:
-        copy.start()
-
+    stride = windows * groups * 4 + 1
     step = 16
 
     def split(value):
@@ -155,10 +146,7 @@
             block = ref[pl.ds(pl.multiple_of(n * step, step), step), :].astype(jnp.float32)
             terms = real_dft([block[:, a * width:(a + 1) * width] for a in range(residues)])
             for g in range(groups):
-                if g == 0:
-                    parts = (terms[0][0], terms[groups][0])
-                else:
-                    parts = terms[g]
+                parts = terms[g] if g else (terms[0][0], terms[groups][0])
                 for side, part in enumerate(parts):
                     hi, lo = split(part)
                     for copy_to in ((0, 1) if own else (which,)):
@@ -200,114 +188,146 @@
         for q in range(4):
             for w in range(windows):
                 start = w * (groups * 4) + g * 4 + q
-                wide[pl.ds(start, width, stride=depth + 1), :] = parts[q][:, w * lanes:(w + 1) * lanes]
+                wide[pl.ds(start, width, stride=stride), :] = parts[q][:, w * lanes:(w + 1) * lanes]
         return carry
 
     lax.fori_loop(0, groups, to_bins, 0, unroll=4)
+
+
+def start_tables(sources, targets, sems):
+    copies = [
+        pltpu.make_async_copy(source, target, sems.at[i])
+        for i, (source, target) in enumerate(zip(sources, targets))
+    ]
+    for copy in copies:
+        copy.start()
+    return copies
+
+
+def cross_bins(own_ref, wide, cross):
+    width, lanes, depth = own_ref.shape
+    channels = lanes // 2
+
+    def one(k, carry):
+        partners = wide[pl.ds(k * (depth + 1), depth), :].astype(jnp.bfloat16)
+        value = jnp.dot(own_ref[k], partners, preferred_element_type=jnp.float32)
+        for part in range(2):
+            cross[pl.ds(part * width + k, channels, stride=2 * width + 1), :] = (
+                value[part * channels:(part + 1) * channels]
+            )
+        return carry
+
+    lax.fori_loop(0, width, one, 0, unroll=8)
+
+
+def own_kernel(windows, *refs):
+    records, (fhi_hbm, flo_hbm, bins_hbm, out_ref, *scratch) = refs[:windows], refs[windows:]
+    *scratch, sems = scratch
+    copies = start_tables((fhi_hbm, flo_hbm, bins_hbm), scratch[:3], sems)
+    whiten_into_bins(True, windows, records, copies, *scratch)
+    wide = scratch[-1]
+    width, lanes, depth = out_ref.shape
+
     def narrow(k, carry):
-        block = wide[pl.ds(k * (depth + 1), depth), :]
-        out_ref[k] = (block.T if own else block).astype(jnp.bfloat16)
+        out_ref[k] = wide[pl.ds(k * (depth + 1), depth), :].T.astype(jnp.bfloat16)
         return carry
 
     lax.fori_loop(0, width, narrow, 0, unroll=8)
 
 
-def prepare(records, windows, tables, own):
-    channels, samples = records[0].shape
-    forward_hi, forward_lo, bins_t = tables
+def first_kernel(windows, *refs):
+    records, (*sources, out_ref), scratch = refs[:2 * windows], refs[2 * windows:2 * windows + 5], refs[2 * windows + 5:]
+    fhi, flo, bins, own_ref, *work, cross, sems = scratch
+    copies = start_tables(sources, scratch[:4], sems)
+    whiten_into_bins(False, windows, records, copies, fhi, flo, bins, *work)
+    copies[3].wait()
+    cross_bins(own_ref, work[-1], cross)
+    rows = 2 * own_ref.shape[0]
+
+    def narrow(i, carry):
+        out_ref[pl.ds(pl.multiple_of(i * rows, rows), rows), :] = (
+            cross[pl.ds(i * (rows + 1), rows), :].astype(jnp.bfloat16)
+        )
+        return carry
+
+    lax.fori_loop(0, out_ref.shape[0] // rows, narrow, 0, unroll=4)
+
+
+def last_kernel(windows, *refs):
+    records, refs = refs[:2 * windows], refs[2 * windows:]
+    sources, (lag_ref, slot_ref, keep_ref, out_hbm), scratch = refs[:5], refs[5:9], refs[9:]
+    fhi, flo, bins, own_ref, early_ref, *work, cross, stage, sems, out_sems = scratch
+    copies = start_tables(sources, scratch[:5], sems)
+    whiten_into_bins(False, windows, records, copies, fhi, flo, bins, *work)
+    copies[3].wait()
+    copies[4].wait()
+    cross_bins(own_ref, work[-1], cross)
+    rows = 2 * own_ref.shape[0]
+    _, offsets, per_out, channels, _ = stage.shape
+    chunks = channels // per_out
+
+    def leave(chunk, slot):
+        target = out_hbm.at[:, pl.ds(chunk * per_out, per_out)]
+        return pltpu.make_async_copy(stage.at[slot], target, out_sems.at[slot])
+
+    def two_chunks(t, carry):
+        for slot in range(2):
+            chunk = t * 2 + slot
+
+            @pl.when(t > 0)
+            def _():
+                leave(chunk - 2, slot).wait()
+
+            def one(n, inner):
+                i = chunk * per_out + n
+                early = early_ref[pl.ds(pl.multiple_of(i * rows, rows), rows), :]
+                late = cross[pl.ds(i * (rows + 1), rows), :].astype(jnp.bfloat16)
+                both = jnp.concatenate([early, late], axis=1)
+                value = jnp.dot(lag_ref[...], both, preferred_element_type=jnp.float32).T
+                for o in range(offsets):
+                    stage[slot, slot_ref[o], n] = value[o * channels:(o + 1) * channels] * keep_ref[o]
+                return inner
+
+            lax.fori_loop(0, per_out, one, 0, unroll=4)
+            leave(chunk, slot).start()
+        return carry
+
+    lax.fori_loop(0, chunks // 2, two_chunks, 0)
+    for slot in range(2):
+        leave(chunks - 2 + slot, slot).wait()
+
+
+def call(kernel, name, windows, operands, tables, extra, out_shape, out_space, buffers=(), signals=()):
+    channels, samples = operands[0].shape
     width = LAGS
     groups = samples // width // 2
     rows = 2 * windows * channels
     depth = windows * groups * 4
     lanes = 2 * channels
-    shape = (width, lanes, depth) if own else (width, depth, lanes)
     any_spec = pl.BlockSpec(memory_space=pl.ANY)
     vmem_spec = pl.BlockSpec(memory_space=pltpu.VMEM)
-    flops = 2 * groups * rows * (3 * 4 * width * width + 8 * width * width)
+    smem_spec = pl.BlockSpec(memory_space=pltpu.SMEM)
+    small = [vmem_spec if v.ndim > 1 else smem_spec for v in extra]
     return pl.pallas_call(
-        functools.partial(prepare_kernel, own, windows),
-        out_shape=jax.ShapeDtypeStruct(shape, jnp.bfloat16),
-        in_specs=[vmem_spec] * len(records) + [any_spec] * 3,
-        out_specs=vmem_spec,
-        scratch_shapes=[
-            pltpu.VMEM(forward_hi.shape, jnp.bfloat16),
-            pltpu.VMEM(forward_lo.shape, jnp.bfloat16),
-            pltpu.VMEM(bins_t.shape, jnp.bfloat16),
+        functools.partial(kernel, windows),
+        out_shape=out_shape,
+        in_specs=[vmem_spec] * len(operands) + [any_spec] * len(tables) + small,
+        out_specs=pl.BlockSpec(memory_space=out_space),
+        scratch_shapes=[pltpu.VMEM(t.shape, jnp.bfloat16) for t in tables] + [
             pltpu.VMEM((groups, rows, 2 * width), jnp.bfloat16),
             pltpu.VMEM((groups, rows, 2 * width), jnp.bfloat16),
             pltpu.VMEM((groups, 2 * width, rows), jnp.float32),
             pltpu.VMEM((width * (depth + 1), lanes), jnp.float32),
-            pltpu.SemaphoreType.DMA((3,)),
+            *buffers,
+            pltpu.SemaphoreType.DMA((len(tables),)),
+            *signals,
         ],
         compiler_params=pltpu.CompilerParams(vmem_limit_bytes=VMEM_LIMIT),
-        cost_estimate=pl.CostEstimate(flops=flops, bytes_accessed=14 * 2**20, transcendentals=0),
-        name="prepare_own" if own else "prepare_partners",
-    )(*records, forward_hi, forward_lo, bins_t)
-
-
-def stack_kernel(chunks, per_chunk, per_out, own_ref, first_ref, second_ref, lag_ref, slot_ref, keep_ref, out_ref, *cross):
-    step = pl.program_id(0)
-    width = LAGS
-    lanes = first_ref.shape[2]
-    channels = lanes // 2
-
-    @pl.when(step < chunks)
-    def _():
-        def one(n, carry):
-            k = step * per_chunk + n
-            partners = jnp.concatenate([first_ref[n], second_ref[n]], axis=1)
-            value = jnp.dot(own_ref[n], partners, preferred_element_type=jnp.float32)
-            for side in range(2):
-                for part in range(2):
-                    cross[side][pl.ds(part * width + k, channels, stride=2 * width + 1), :] = (
-                        value[part * channels:(part + 1) * channels, side * lanes:(side + 1) * lanes]
-                    )
-            return carry
-
-        lax.fori_loop(0, per_chunk, one, 0, unroll=8)
-
-    @pl.when(step >= chunks)
-    def _():
-        def one(n, carry):
-            i = (step - chunks) * per_out + n
-            part = pl.ds(i * (2 * width + 1), 2 * width)
-            block = jnp.concatenate([ref[part, :].astype(jnp.bfloat16) for ref in cross], axis=1)
-            value = jnp.dot(lag_ref[...], block, preferred_element_type=jnp.float32).T
-            for o in range(out_ref.shape[0]):
-                out_ref[slot_ref[o], n] = value[o * channels:(o + 1) * channels] * keep_ref[o]
-            return carry
-
-        lax.fori_loop(0, per_out, one, 0, unroll=4)
-
-
-def stack(own, first, second, lag_t, slots, keep):
-    width, lanes, depth = own.shape
-    channels = lanes // 2
-    chunks, out_chunks = 4, 8
-    per_chunk, per_out = width // chunks, channels // out_chunks
-    block = lambda s: (jnp.minimum(s, chunks - 1), 0, 0)
-    offsets = keep.shape[0]
-    return pl.pallas_call(
-        functools.partial(stack_kernel, chunks, per_chunk, per_out),
-        grid=(chunks + out_chunks,),
-        out_shape=jax.ShapeDtypeStruct((offsets, channels, channels, LAGS), jnp.float32),
-        in_specs=[
-            pl.BlockSpec((per_chunk, lanes, depth), block),
-            pl.BlockSpec((per_chunk, depth, lanes), block),
-            pl.BlockSpec((per_chunk, depth, lanes), block),
-            pl.BlockSpec(lag_t.shape, lambda s: (0, 0)),
-            pl.BlockSpec(memory_space=pltpu.SMEM),
-            pl.BlockSpec(memory_space=pltpu.SMEM),
-        ],
-        out_specs=pl.BlockSpec(
-            (offsets, per_out, channels, LAGS), lambda s: (0, jnp.maximum(s - chunks, 0), 0, 0)
+        cost_estimate=pl.CostEstimate(
+            flops=20 * groups * rows * 4 * width * width, bytes_accessed=14 * 2**20, transcendentals=0
         ),
-        scratch_shapes=[pltpu.VMEM((channels * (2 * width + 1), lanes), jnp.float32)] * 2,
-        compiler_params=pltpu.CompilerParams(
-            vmem_limit_bytes=VMEM_LIMIT, dimension_semantics=("arbitrary",)
-        ),
-        name="stack_lags",
-    )(own, first, second, lag_t, slots, keep)
+        name=name,
+    )(*operands, *tables, *extra)
 
 
 def per_device(traces, live, reach):
@@ -347,20 +367,43 @@
         across = send(across_payload, lambda q, p, c, g: (q + p * g, 1 - p, c, g))
         return jnp.where(place == 0, mine, upper), beside, across
 
+    width = LAGS
+    lanes = 2 * channels
+    depth = windows * samples // width * 2
+    crossed = pltpu.VMEM((channels * (2 * width + 1), lanes), jnp.float32)
+    own_tables = (forward_hi, forward_lo, jnp.asarray(bins_t[1]))
+    tables = (forward_hi, forward_lo, jnp.asarray(bins_t[0]))
+
     upper = [send(mine, lambda q, p, c, g: (q + 1, p, c, g)) for mine in masked]
-    own = prepare(masked, windows, (forward_hi, forward_lo, jnp.asarray(bins_t[1])), True)
+    own = call(
+        own_kernel, "own_bins", windows, masked, own_tables, (),
+        jax.ShapeDtypeStruct((width, lanes, depth), jnp.bfloat16), pltpu.VMEM,
+    )
     upper[0], own = lax.optimization_barrier((upper[0], own))
-    here, beside, across = map(list, zip(*(from_neighbours(mine, up) for mine, up in zip(masked, upper))))
-    partner_tables = (forward_hi, forward_lo, jnp.asarray(bins_t[0]))
-    across[0], beside[-1] = lax.optimization_barrier((across[0], beside[-1]))
-    first = prepare(here + beside, windows, partner_tables, False)
-    across[-1], first = lax.optimization_barrier((across[-1], first))
+    here, beside, across = [], [], []
+    for w in range(windows):
+        if w:
+            upper[w], beside[w - 1], across[w - 1] = lax.optimization_barrier(
+                (upper[w], beside[w - 1], across[w - 1])
+            )
+        for known, new in zip((here, beside, across), from_neighbours(masked[w], upper[w])):
+            known.append(new)
+    early = call(
+        first_kernel, "first_pair", windows, here + beside, (*tables, own), (),
+        jax.ShapeDtypeStruct((channels * 2 * width, lanes), jnp.bfloat16), pltpu.VMEM, (crossed,),
+    )
+    *across, early = lax.optimization_barrier((*across, early))
     across_beside = [send(block, lambda q, p, c, g: (q, p, 1 - c, g)) for block in across]
-    second = prepare(across + across_beside, windows, partner_tables, False)
     slots = jnp.stack([0, 1 + 2 * core, 2, 3 - 2 * core]).astype(jnp.int32)
     offset_ids = place * owned + slots
     keep = jnp.where(offset_ids < reach[0], jnp.float32(scale), jnp.float32(0.0))
-    return stack(own, first, second, jnp.asarray(lag_t), slots, keep)[None]
+    result = call(
+        last_kernel, "second_pair", windows, across + across_beside, (*tables, own, early),
+        (jnp.asarray(lag_t), slots, keep),
+        jax.ShapeDtypeStruct((owned, channels, channels, LAGS), jnp.float32), pl.ANY,
+        (crossed, pltpu.VMEM((2, owned, channels // 8, channels, LAGS), jnp.float32)), (pltpu.SemaphoreType.DMA((2,)),),
+    )
+    return result[None]
 
 
 def solution(mesh):

time: 87.8 us -> 85 us (0.968)
  the two profiles are of different devices: /device:TPU:21 before, /device:TPU:19 now
where the time goes in v2:
time: 85 us; the launch traced here: 84.7 us
  Pallas kernels  41.2 us (48%)
  waiting for transfers between devices  22.3 us (26%)
  starting transfers between devices  16.5 us (19%)
  other arithmetic  2.29 us (3%)
  local copies, waits for them, and re-layouts  1.59 us (2%)
    pallas_call x3, Pallas kernels, call(): pl.pallas_call(functools.partial(kernel, windows), out_shape=out_shape, i...  41.2 us
    ppermute x8, waiting for transfers between devices, send(): return lax.ppermute(payload, ('fibre', 'freq'), pairs)  22.3 us
    ppermute x8, starting transfers between devices, send(): return lax.ppermute(payload, ('fibre', 'freq'), pairs)  16.5 us
  transfers between devices with their start and end apart: 8, of which 5 were waited for; matrix products, arithmetic and copies ran while one was open for 0% of the time, Pallas kernels for 27%

profile of v2, /device:TPU:19, one launch (start us, length us, event | category | flops | bytes accessed | tf_op | source)
XLA Modules:
  0.0 84.7 jit_solution(5435531256069716443)
XLA Ops:
  0.0 0.7 convert_element_type.3
  0.7 1.3 %bitcast_multiply_fusion = (bf16[64,4096]{1,0:T(8,128)(2,1)S(1)}, bf16[64,4096]{1,0:T(8,128)(2,1)S(1)}) fusion(bf16[2,64,4096]{2,1,0:T(8,128)(2,1)} %param.8, bf16[64]{0:T(256)(128)(2,1)S(1)} %convert_element_type.3), kind=kLoop, calls=%fused_computation | loop fusion | flops 524288 | bytes 2097280 | tf_op jit(solution)/shard_map/mul | solution.py:342
  2.0 2.1 %collective-permute-start.1 = (bf16[64,4096]{1,0:T(8,128)(2,1)S(1)}, bf16[64,4096]{1,0:T(8,128)(2,1)S(1)}, u32[]{:S(2)}, u32[]{:S(2)}) collective-permute-start(bf16[64,4096]{1,0:T(8,128)(2,1)S(1)} %get-tuple-element.23.refs_0_), channel_id=1, source_target_pairs={{8,0},{9,1},{10,2},{11,3},{12,4},{13,5},{14,6},{15,7},{16,8},{17,9... | collective-permute-start | bytes 1572872 | tf_op jit(solution)/shard_map/ppermute | solution.py:361
  4.1 2.1 %collective-permute-start = (bf16[64,4096]{1,0:T(8,128)(2,1)S(1)}, bf16[64,4096]{1,0:T(8,128)(2,1)S(1)}, u32[]{:S(2)}, u32[]{:S(2)}) collective-permute-start(bf16[64,4096]{1,0:T(8,128)(2,1)S(1)} %get-tuple-element.24.refs_1_), channel_id=1, source_target_pairs={{8,0},{9,1},{10,2},{11,3},{12,4},{13,5},{14,6},{15,7},{16,8},{17,9... | collective-permute-start | bytes 1572872 | tf_op jit(solution)/shard_map/ppermute | solution.py:361
  6.2 0.0 copy-start
  6.2 1.6 %copy-done = bf16[16,256,256]{2,1,0:T(8,128)(2,1)S(1)} copy-done((bf16[16,256,256]{2,1,0:T(8,128)(2,1)S(1)}, bf16[16,256,256]{2,1,0:T(8,128)(2,1)}, u32[]{:S(2)}) %copy-start) | copy-done | bytes 2097176
  7.8 10.2 %own_bins.1.refs_7_ = bf16[128,128,128]{2,1,0:T(8,128)(2,1)} custom-call(bf16[64,4096]{1,0:T(8,128)(2,1)S(1)} %get-tuple-element.23.refs_0_, bf16[64,4096]{1,0:T(8,128)(2,1)S(1)} %get-tuple-element.24.refs_1_, bf16[16,256,256]{2,1,0:T(8,128)(2,1)S(1)} %copy-done, bf16[16,256,256]{2,1,0:T(8,128)(2,1)} %constant.64.clone.refs_3_.refs_5_, ...), custom_call_target="tpu_custom_call" | custom-call | flops 5368709120 | bytes 14680064 | tf_op jit(solution)/shard_map/own_bins/pallas_call | solution.py:311
  18.1 0.0 collective-permute-done.1
  18.1 0.1 broadcast_select_fusion.1
  18.2 2.0 %collective-permute-start.3 = (bf16[64,4096]{1,0:T(8,128)(2,1)S(1)}, bf16[64,4096]{1,0:T(8,128)(2,1)S(1)}, u32[]{:S(2)}, u32[]{:S(2)}) collective-permute-start(bf16[64,4096]{1,0:T(8,128)(2,1)S(1)} %get-tuple-element.29), channel_id=1, source_target_pairs={{4,0},{5,1},{6,2},{7,3},{0,4},{9,5},{2,6},{11,7},{12,8},{13,9},{14... | collective-permute-start | bytes 1572872 | tf_op jit(solution)/shard_map/ppermute | solution.py:361
  20.2 3.6 %collective-permute-start.2 = (bf16[64,4096]{1,0:T(8,128)(2,1)S(1)}, bf16[64,4096]{1,0:T(8,128)(2,1)S(1)}, u32[]{:S(2)}, u32[]{:S(2)}) collective-permute-start(bf16[64,4096]{1,0:T(8,128)(2,1)S(1)} %get-tuple-element.30), channel_id=1, source_target_pairs={{2,0},{3,1},{1,2},{8,3},{6,4},{7,5},{5,6},{12,7},{10,8},{11,9},{9,... | collective-permute-start | bytes 1572872 | tf_op jit(solution)/shard_map/ppermute | solution.py:361
  23.9 4.1 %collective-permute-done = bf16[64,4096]{1,0:T(8,128)(2,1)S(1)} collective-permute-done((bf16[64,4096]{1,0:T(8,128)(2,1)S(1)}, bf16[64,4096]{1,0:T(8,128)(2,1)S(1)}, u32[]{:S(2)}, u32[]{:S(2)}) %collective-permute-start) | collective-permute-done | bytes 524320 | tf_op jit(solution)/shard_map/ppermute | solution.py:361
  27.9 4.3 %collective-permute-done.3.refs_0_ = bf16[64,4096]{1,0:T(8,128)(2,1)S(1)} collective-permute-done((bf16[64,4096]{1,0:T(8,128)(2,1)S(1)}, bf16[64,4096]{1,0:T(8,128)(2,1)S(1)}, u32[]{:S(2)}, u32[]{:S(2)}) %collective-permute-start.3) | collective-permute-done | bytes 524320 | tf_op jit(solution)/shard_map/ppermute | solution.py:361
  32.2 0.0 collective-permute-done.2.refs_2_
  32.2 0.1 broadcast_select_fusion.4
  32.3 4.1 %collective-permute-start.5 = (bf16[64,4096]{1,0:T(8,128)(2,1)S(1)}, bf16[64,4096]{1,0:T(8,128)(2,1)S(1)}, u32[]{:S(2)}, u32[]{:S(2)}) collective-permute-start(bf16[64,4096]{1,0:T(8,128)(2,1)S(1)} %get-tuple-element.25), channel_id=1, source_target_pairs={{2,0},{3,1},{1,2},{8,3},{6,4},{7,5},{5,6},{12,7},{10,8},{11,9},{9,... | collective-permute-start | bytes 1572872 | tf_op jit(solution)/shard_map/ppermute | solution.py:361
  36.5 2.0 %collective-permute-start.4 = (bf16[64,4096]{1,0:T(8,128)(2,1)S(1)}, bf16[64,4096]{1,0:T(8,128)(2,1)S(1)}, u32[]{:S(2)}, u32[]{:S(2)}) collective-permute-start(bf16[64,4096]{1,0:T(8,128)(2,1)S(1)} %get-tuple-element.27), channel_id=1, source_target_pairs={{4,0},{5,1},{6,2},{7,3},{0,4},{9,5},{2,6},{11,7},{12,8},{13,9},{14... | collective-permute-start | bytes 1572872 | tf_op jit(solution)/shard_map/ppermute | solution.py:361
  38.5 12.5 %collective-permute-done.5.refs_3_ = bf16[64,4096]{1,0:T(8,128)(2,1)S(1)} collective-permute-done((bf16[64,4096]{1,0:T(8,128)(2,1)S(1)}, bf16[64,4096]{1,0:T(8,128)(2,1)S(1)}, u32[]{:S(2)}, u32[]{:S(2)}) %collective-permute-start.5) | collective-permute-done | bytes 524320 | tf_op jit(solution)/shard_map/ppermute | solution.py:361
  51.0 0.0 copy-start.1
  51.0 12.6 %first_pair.1.refs_8_ = bf16[16384,128]{1,0:T(8,128)(2,1)} custom-call(bf16[64,4096]{1,0:T(8,128)(2,1)S(1)} %get-tuple-element.28.refs_0_, bf16[64,4096]{1,0:T(8,128)(2,1)S(1)} %get-tuple-element.26.refs_1_, bf16[64,4096]{1,0:T(8,128)(2,1)S(1)} %collective-permute-done.2.refs_2_, bf16[64,4096]{1,0:T(8,128)(2,1)S(1)} %collective-permute-done.5.refs_3_, ...), custom_call_target="tpu_custom_call" | custom-call | flops 5368709120 | bytes 14680064 | tf_op jit(solution)/shard_map/first_pair/pallas_call | solution.py:311
  63.5 0.0 collective-permute-done.4.refs_1_
  63.6 0.1 collective-permute-start.6
  63.6 0.5 collective-permute-start.7
  64.8 0.1 compare_select_fusion
  64.9 0.7 collective-permute-done.6.refs_2_
  65.5 0.7 collective-permute-done.7.refs_3_
  66.3 0.0 copy-done.1
  66.3 18.4 %second_pair.1 = f32[4,64,64,128]{3,2,1,0:T(8,128)} custom-call(bf16[64,4096]{1,0:T(8,128)(2,1)S(1)} %collective-permute-done.3.refs_0_, bf16[64,4096]{1,0:T(8,128)(2,1)S(1)} %collective-permute-done.4.refs_1_, bf16[64,4096]{1,0:T(8,128)(2,1)S(1)} %collective-permute-done.6.refs_2_, bf16[64,4096]{1,0:T(8,128)(2,1)S(1)} %collective-permute-done.7.refs_3_, ...), custom_call_target="tpu_custom_call" | custom-call | flops 5368709120 | bytes 14680064 | tf_op jit(solution)/shard_map/second_pair/pallas_call | solution.py:311
Async XLA Ops:
  2.0 16.1 %collective-permute-start.1 = (bf16[64,4096]{1,0:T(8,128)(2,1)S(1)}, bf16[64,4096]{1,0:T(8,128)(2,1)S(1)}, u32[]{:S(2)}, u32[]{:S(2)}) collective-permute-start(bf16[64,4096]{1,0:T(8,128)(2,1)S(1)} %get-tuple-element.23.refs_0_), channel_id=1, source_target_pairs={{8,0},{9,1},{10,2},{11,3},{12,4},{13,5},{14,6},{15,7},{16,8},{17,9... | collective-permute-start | bytes 1572872 | tf_op jit(solution)/shard_map/ppermute | solution.py:361
  4.1 23.8 %collective-permute-start = (bf16[64,4096]{1,0:T(8,128)(2,1)S(1)}, bf16[64,4096]{1,0:T(8,128)(2,1)S(1)}, u32[]{:S(2)}, u32[]{:S(2)}) collective-permute-start(bf16[64,4096]{1,0:T(8,128)(2,1)S(1)} %get-tuple-element.24.refs_1_), channel_id=1, source_target_pairs={{8,0},{9,1},{10,2},{11,3},{12,4},{13,5},{14,6},{15,7},{16,8},{17,9... | collective-permute-start | bytes 1572872 | tf_op jit(solution)/shard_map/ppermute | solution.py:361
  6.2 1.6 %copy-start = (bf16[16,256,256]{2,1,0:T(8,128)(2,1)S(1)}, bf16[16,256,256]{2,1,0:T(8,128)(2,1)}, u32[]{:S(2)}) copy-start(bf16[16,256,256]{2,1,0:T(8,128)(2,1)} %constant.63.clone.refs_2_.refs_4_) | copy-start | bytes 6291460
  18.2 14.0 %collective-permute-start.3 = (bf16[64,4096]{1,0:T(8,128)(2,1)S(1)}, bf16[64,4096]{1,0:T(8,128)(2,1)S(1)}, u32[]{:S(2)}, u32[]{:S(2)}) collective-permute-start(bf16[64,4096]{1,0:T(8,128)(2,1)S(1)} %get-tuple-element.29), channel_id=1, source_target_pairs={{4,0},{5,1},{6,2},{7,3},{0,4},{9,5},{2,6},{11,7},{12,8},{13,9},{14... | collective-permute-start | bytes 1572872 | tf_op jit(solution)/shard_map/ppermute | solution.py:361
  20.2 12.0 %collective-permute-start.2 = (bf16[64,4096]{1,0:T(8,128)(2,1)S(1)}, bf16[64,4096]{1,0:T(8,128)(2,1)S(1)}, u32[]{:S(2)}, u32[]{:S(2)}) collective-permute-start(bf16[64,4096]{1,0:T(8,128)(2,1)S(1)} %get-tuple-element.30), channel_id=1, source_target_pairs={{2,0},{3,1},{1,2},{8,3},{6,4},{7,5},{5,6},{12,7},{10,8},{11,9},{9,... | collective-permute-start | bytes 1572872 | tf_op jit(solution)/shard_map/ppermute | solution.py:361
  32.3 18.6 %collective-permute-start.5 = (bf16[64,4096]{1,0:T(8,128)(2,1)S(1)}, bf16[64,4096]{1,0:T(8,128)(2,1)S(1)}, u32[]{:S(2)}, u32[]{:S(2)}) collective-permute-start(bf16[64,4096]{1,0:T(8,128)(2,1)S(1)} %get-tuple-element.25), channel_id=1, source_target_pairs={{2,0},{3,1},{1,2},{8,3},{6,4},{7,5},{5,6},{12,7},{10,8},{11,9},{9,... | collective-permute-start | bytes 1572872 | tf_op jit(solution)/shard_map/ppermute | solution.py:361
  36.5 27.1 %collective-permute-start.4 = (bf16[64,4096]{1,0:T(8,128)(2,1)S(1)}, bf16[64,4096]{1,0:T(8,128)(2,1)S(1)}, u32[]{:S(2)}, u32[]{:S(2)}) collective-permute-start(bf16[64,4096]{1,0:T(8,128)(2,1)S(1)} %get-tuple-element.27), channel_id=1, source_target_pairs={{4,0},{5,1},{6,2},{7,3},{0,4},{9,5},{2,6},{11,7},{12,8},{13,9},{14... | collective-permute-start | bytes 1572872 | tf_op jit(solution)/shard_map/ppermute | solution.py:361
  51.0 15.3 %copy-start.1 = (bf16[128,256]{1,0:T(8,128)(2,1)S(1)}, bf16[128,256]{1,0:T(8,128)(2,1)}, u32[]{:S(2)}) copy-start(bf16[128,256]{1,0:T(8,128)(2,1)} %constant.67.clone.refs_9_) | copy-start | bytes 196612
  63.6 2.0 %collective-permute-start.6 = (bf16[64,4096]{1,0:T(8,128)(2,1)S(1)}, bf16[64,4096]{1,0:T(8,128)(2,1)S(1)}, u32[]{:S(2)}, u32[]{:S(2)}) collective-permute-start(bf16[64,4096]{1,0:T(8,128)(2,1)S(1)} %collective-permute-done.3.refs_0_), channel_id=1, source_target_pairs={{2,0},{3,1},{0,2},{1,3},{6,4},{7,5},{4,6},{5,7},{10,8},{11,9},{8,1... | collective-permute-start | bytes 1572872 | tf_op jit(solution)/shard_map/ppermute | solution.py:361
  63.6 2.6 %collective-permute-start.7 = (bf16[64,4096]{1,0:T(8,128)(2,1)S(1)}, bf16[64,4096]{1,0:T(8,128)(2,1)S(1)}, u32[]{:S(2)}, u32[]{:S(2)}) collective-permute-start(bf16[64,4096]{1,0:T(8,128)(2,1)S(1)} %collective-permute-done.4.refs_1_), channel_id=1, source_target_pairs={{2,0},{3,1},{0,2},{1,3},{6,4},{7,5},{4,6},{5,7},{10,8},{11,9},{8,1... | collective-permute-start | bytes 1572872 | tf_op jit(solution)/shard_map/ppermute | solution.py:361

commit v3 on v2

--- a/solution.py
+++ b/solution.py
@@ -169,7 +169,7 @@
         squared = (value * value).reshape(2 * width // bands, bands, rows)
         return power + squared.sum(0)
 
-    power = lax.fori_loop(0, groups, forward, jnp.zeros((bands, rows), jnp.float32), unroll=4)
+    power = lax.fori_loop(0, groups, forward, jnp.zeros((bands, rows), jnp.float32), unroll=8)
     gain = 1.0 / jnp.sqrt(power * (1.0 / BAND) + 1e-6)
     copies[2].wait()
 
@@ -191,7 +191,7 @@
                 wide[pl.ds(start, width, stride=stride), :] = parts[q][:, w * lanes:(w + 1) * lanes]
         return carry
 
-    lax.fori_loop(0, groups, to_bins, 0, unroll=4)
+    lax.fori_loop(0, groups, to_bins, 0, unroll=8)
 
 
 def start_tables(sources, targets, sems):
@@ -217,7 +217,7 @@
             )
         return carry
 
-    lax.fori_loop(0, width, one, 0, unroll=8)
+    lax.fori_loop(0, width, one, 0, unroll=16)
 
 
 def own_kernel(windows, *refs):
@@ -288,7 +288,7 @@
                     stage[slot, slot_ref[o], n] = value[o * channels:(o + 1) * channels] * keep_ref[o]
                 return inner
 
-            lax.fori_loop(0, per_out, one, 0, unroll=4)
+            lax.fori_loop(0, per_out, one, 0, unroll=8)
             leave(chunk, slot).start()
         return carry
 
@@ -338,8 +338,7 @@
     place = lax.axis_index("freq")
     forward_hi, forward_lo, bins_t, lag_t, scale = build_tables(samples)
     forward_hi, forward_lo = jnp.asarray(forward_hi), jnp.asarray(forward_lo)
-    alive = live.astype(traces.dtype)[:, None]
-    masked = [traces[w] * alive for w in range(windows)]
+    masked = [jnp.where(live[:, None] > 0, traces[w], jnp.zeros((), traces.dtype)) for w in range(windows)]
 
     quads = blocks // owned
     half = owned // 2
@@ -383,11 +382,10 @@
     here, beside, across = [], [], []
     for w in range(windows):
         if w:
-            upper[w], beside[w - 1], across[w - 1] = lax.optimization_barrier(
-                (upper[w], beside[w - 1], across[w - 1])
-            )
+            upper[w], beside[w - 1] = lax.optimization_barrier((upper[w], beside[w - 1]))
         for known, new in zip((here, beside, across), from_neighbours(masked[w], upper[w])):
             known.append(new)
+    across[0], beside[-1] = lax.optimization_barrier((across[0], beside[-1]))
     early = call(
         first_kernel, "first_pair", windows, here + beside, (*tables, own), (),
         jax.ShapeDtypeStruct((channels * 2 * width, lanes), jnp.bfloat16), pltpu.VMEM, (crossed,),

time: 85 us -> 75.6 us (0.89)
  the two profiles are of different devices: /device:TPU:19 before, /device:TPU:21 now
where the time goes in v3:
time: 75.6 us; the launch traced here: 74.7 us
  Pallas kernels  35.6 us (47%)
  waiting for transfers between devices  17.5 us (23%)
  starting transfers between devices  16.8 us (22%)
  other arithmetic  2.3 us (3%)
  local copies, waits for them, and re-layouts  1.59 us (2%)
  between operations  0.83 us (1%)
    pallas_call x3, Pallas kernels, call(): pl.pallas_call(functools.partial(kernel, windows), out_shape=out_shape, i...  35.6 us
    ppermute x8, waiting for transfers between devices, send(): return lax.ppermute(payload, ('fibre', 'freq'), pairs)  17.5 us
    ppermute x8, starting transfers between devices, send(): return lax.ppermute(payload, ('fibre', 'freq'), pairs)  16.8 us
    unnamed x4, local copies, waits for them, and re-layouts  1.59 us
  transfers between devices with their start and end apart: 8, of which 5 were waited for; matrix products, arithmetic and copies ran while one was open for 0% of the time, Pallas kernels for 27%

profile of v3, /device:TPU:21, one launch (start us, length us, event | category | flops | bytes accessed | tf_op | source)
XLA Modules:
  0.0 74.7 jit_solution(6558324294579549997)
XLA Ops:
  0.0 0.7 broadcast_compare_fusion
  0.7 1.3 %bitcast_select_fusion = (bf16[64,4096]{1,0:T(8,128)(2,1)S(1)}, bf16[64,4096]{1,0:T(8,128)(2,1)S(1)}) fusion(bf16[2,64,4096]{2,1,0:T(8,128)(2,1)} %param.8, pred[64]{0:T(512)(128)(4,1)S(1)} %broadcast_compare_fusion), kind=kLoop, calls=%fused_computation | loop fusion | flops 524288 | bytes 2097216 | tf_op jit(solution)/shard_map/jit(_where)/select_n | solution.py:341
  2.0 2.1 %collective-permute-start = (bf16[64,4096]{1,0:T(8,128)(2,1)S(1)}, bf16[64,4096]{1,0:T(8,128)(2,1)S(1)}, u32[]{:S(2)}, u32[]{:S(2)}) collective-permute-start(bf16[64,4096]{1,0:T(8,128)(2,1)S(1)} %get-tuple-element.26.refs_0_), channel_id=1, source_target_pairs={{8,0},{9,1},{10,2},{11,3},{12,4},{13,5},{14,6},{15,7},{16,8},{17,9... | collective-permute-start | bytes 1572872 | tf_op jit(solution)/shard_map/ppermute | solution.py:360
  4.1 2.1 %collective-permute-start.2 = (bf16[64,4096]{1,0:T(8,128)(2,1)S(1)}, bf16[64,4096]{1,0:T(8,128)(2,1)S(1)}, u32[]{:S(2)}, u32[]{:S(2)}) collective-permute-start(bf16[64,4096]{1,0:T(8,128)(2,1)S(1)} %get-tuple-element.25.refs_1_), channel_id=1, source_target_pairs={{8,0},{9,1},{10,2},{11,3},{12,4},{13,5},{14,6},{15,7},{16,8},{17,9... | collective-permute-start | bytes 1572872 | tf_op jit(solution)/shard_map/ppermute | solution.py:360
  6.2 0.0 copy-start
  6.2 1.6 %copy-done = bf16[16,256,256]{2,1,0:T(8,128)(2,1)S(1)} copy-done((bf16[16,256,256]{2,1,0:T(8,128)(2,1)S(1)}, bf16[16,256,256]{2,1,0:T(8,128)(2,1)}, u32[]{:S(2)}) %copy-start) | copy-done | bytes 2097176
  7.8 9.6 %own_bins.1.refs_7_ = bf16[128,128,128]{2,1,0:T(8,128)(2,1)} custom-call(bf16[64,4096]{1,0:T(8,128)(2,1)S(1)} %get-tuple-element.26.refs_0_, bf16[64,4096]{1,0:T(8,128)(2,1)S(1)} %get-tuple-element.25.refs_1_, bf16[16,256,256]{2,1,0:T(8,128)(2,1)S(1)} %copy-done, bf16[16,256,256]{2,1,0:T(8,128)(2,1)} %constant.67.clone.refs_3_.refs_5_, ...), custom_call_target="tpu_custom_call" | custom-call | flops 5368709120 | bytes 14680064 | tf_op jit(solution)/shard_map/own_bins/pallas_call | solution.py:311
  17.4 0.0 collective-permute-done
  17.4 0.1 broadcast_select_fusion.1
  17.5 3.9 %collective-permute-start.3 = (bf16[64,4096]{1,0:T(8,128)(2,1)S(1)}, bf16[64,4096]{1,0:T(8,128)(2,1)S(1)}, u32[]{:S(2)}, u32[]{:S(2)}) collective-permute-start(bf16[64,4096]{1,0:T(8,128)(2,1)S(1)} %get-tuple-element.31), channel_id=1, source_target_pairs={{2,0},{3,1},{1,2},{8,3},{6,4},{7,5},{5,6},{12,7},{10,8},{11,9},{9,... | collective-permute-start | bytes 1572872 | tf_op jit(solution)/shard_map/ppermute | solution.py:360
  21.4 3.0 %collective-permute-start.1 = (bf16[64,4096]{1,0:T(8,128)(2,1)S(1)}, bf16[64,4096]{1,0:T(8,128)(2,1)S(1)}, u32[]{:S(2)}, u32[]{:S(2)}) collective-permute-start(bf16[64,4096]{1,0:T(8,128)(2,1)S(1)} %get-tuple-element.32), channel_id=1, source_target_pairs={{4,0},{5,1},{6,2},{7,3},{0,4},{9,5},{2,6},{11,7},{12,8},{13,9},{14... | collective-permute-start | bytes 1572872 | tf_op jit(solution)/shard_map/ppermute | solution.py:360
  24.4 3.5 %collective-permute-done.2 = bf16[64,4096]{1,0:T(8,128)(2,1)S(1)} collective-permute-done((bf16[64,4096]{1,0:T(8,128)(2,1)S(1)}, bf16[64,4096]{1,0:T(8,128)(2,1)S(1)}, u32[]{:S(2)}, u32[]{:S(2)}) %collective-permute-start.2) | collective-permute-done | bytes 524320 | tf_op jit(solution)/shard_map/ppermute | solution.py:360
  27.9 6.4 %collective-permute-done.3.refs_2_ = bf16[64,4096]{1,0:T(8,128)(2,1)S(1)} collective-permute-done((bf16[64,4096]{1,0:T(8,128)(2,1)S(1)}, bf16[64,4096]{1,0:T(8,128)(2,1)S(1)}, u32[]{:S(2)}, u32[]{:S(2)}) %collective-permute-start.3) | collective-permute-done | bytes 524320 | tf_op jit(solution)/shard_map/ppermute | solution.py:360
  34.3 0.1 broadcast_select_fusion
  34.5 1.9 %collective-permute-start.4 = (bf16[64,4096]{1,0:T(8,128)(2,1)S(1)}, bf16[64,4096]{1,0:T(8,128)(2,1)S(1)}, u32[]{:S(2)}, u32[]{:S(2)}) collective-permute-start(bf16[64,4096]{1,0:T(8,128)(2,1)S(1)} %get-tuple-element.29), channel_id=1, source_target_pairs={{2,0},{3,1},{1,2},{8,3},{6,4},{7,5},{5,6},{12,7},{10,8},{11,9},{9,... | collective-permute-start | bytes 1572872 | tf_op jit(solution)/shard_map/ppermute | solution.py:360
  36.4 3.3 %collective-permute-start.5 = (bf16[64,4096]{1,0:T(8,128)(2,1)S(1)}, bf16[64,4096]{1,0:T(8,128)(2,1)S(1)}, u32[]{:S(2)}, u32[]{:S(2)}) collective-permute-start(bf16[64,4096]{1,0:T(8,128)(2,1)S(1)} %get-tuple-element.28), channel_id=1, source_target_pairs={{4,0},{5,1},{6,2},{7,3},{0,4},{9,5},{2,6},{11,7},{12,8},{13,9},{14... | collective-permute-start | bytes 1572872 | tf_op jit(solution)/shard_map/ppermute | solution.py:360
  39.7 0.0 collective-permute-done.1.refs_0_
  39.7 6.2 %collective-permute-done.4.refs_3_ = bf16[64,4096]{1,0:T(8,128)(2,1)S(1)} collective-permute-done((bf16[64,4096]{1,0:T(8,128)(2,1)S(1)}, bf16[64,4096]{1,0:T(8,128)(2,1)S(1)}, u32[]{:S(2)}, u32[]{:S(2)}) %collective-permute-start.4) | collective-permute-done | bytes 524320 | tf_op jit(solution)/shard_map/ppermute | solution.py:360
  45.9 0.0 copy-start.1
  45.9 10.7 %first_pair.1.refs_8_ = bf16[16384,128]{1,0:T(8,128)(2,1)} custom-call(bf16[64,4096]{1,0:T(8,128)(2,1)S(1)} %get-tuple-element.30.refs_0_, bf16[64,4096]{1,0:T(8,128)(2,1)S(1)} %get-tuple-element.27.refs_1_, bf16[64,4096]{1,0:T(8,128)(2,1)S(1)} %collective-permute-done.3.refs_2_, bf16[64,4096]{1,0:T(8,128)(2,1)S(1)} %collective-permute-done.4.refs_3_, ...), custom_call_target="tpu_custom_call" | custom-call | flops 5368709120 | bytes 14680064 | tf_op jit(solution)/shard_map/first_pair/pallas_call | solution.py:311
  56.5 0.0 collective-permute-done.5.refs_1_
  56.5 0.1 collective-permute-start.6
  56.6 0.5 collective-permute-start.7
  57.8 0.1 compare_select_fusion
  57.8 0.7 collective-permute-done.6.refs_2_
  58.5 0.7 %collective-permute-done.7.refs_3_ = bf16[64,4096]{1,0:T(8,128)(2,1)S(1)} collective-permute-done((bf16[64,4096]{1,0:T(8,128)(2,1)S(1)}, bf16[64,4096]{1,0:T(8,128)(2,1)S(1)}, u32[]{:S(2)}, u32[]{:S(2)}) %collective-permute-start.7) | collective-permute-done | bytes 524320 | tf_op jit(solution)/shard_map/ppermute | solution.py:360
  59.3 0.0 copy-done.1
  59.3 15.4 %second_pair.1 = f32[4,64,64,128]{3,2,1,0:T(8,128)} custom-call(bf16[64,4096]{1,0:T(8,128)(2,1)S(1)} %collective-permute-done.1.refs_0_, bf16[64,4096]{1,0:T(8,128)(2,1)S(1)} %collective-permute-done.5.refs_1_, bf16[64,4096]{1,0:T(8,128)(2,1)S(1)} %collective-permute-done.6.refs_2_, bf16[64,4096]{1,0:T(8,128)(2,1)S(1)} %collective-permute-done.7.refs_3_, ...), custom_call_target="tpu_custom_call" | custom-call | flops 5368709120 | bytes 14680064 | tf_op jit(solution)/shard_map/second_pair/pallas_call | solution.py:311
Async XLA Ops:
  2.0 15.4 %collective-permute-start = (bf16[64,4096]{1,0:T(8,128)(2,1)S(1)}, bf16[64,4096]{1,0:T(8,128)(2,1)S(1)}, u32[]{:S(2)}, u32[]{:S(2)}) collective-permute-start(bf16[64,4096]{1,0:T(8,128)(2,1)S(1)} %get-tuple-element.26.refs_0_), channel_id=1, source_target_pairs={{8,0},{9,1},{10,2},{11,3},{12,4},{13,5},{14,6},{15,7},{16,8},{17,9... | collective-permute-start | bytes 1572872 | tf_op jit(solution)/shard_map/ppermute | solution.py:360
  4.1 23.8 %collective-permute-start.2 = (bf16[64,4096]{1,0:T(8,128)(2,1)S(1)}, bf16[64,4096]{1,0:T(8,128)(2,1)S(1)}, u32[]{:S(2)}, u32[]{:S(2)}) collective-permute-start(bf16[64,4096]{1,0:T(8,128)(2,1)S(1)} %get-tuple-element.25.refs_1_), channel_id=1, source_target_pairs={{8,0},{9,1},{10,2},{11,3},{12,4},{13,5},{14,6},{15,7},{16,8},{17,9... | collective-permute-start | bytes 1572872 | tf_op jit(solution)/shard_map/ppermute | solution.py:360
  6.2 1.6 %copy-start = (bf16[16,256,256]{2,1,0:T(8,128)(2,1)S(1)}, bf16[16,256,256]{2,1,0:T(8,128)(2,1)}, u32[]{:S(2)}) copy-start(bf16[16,256,256]{2,1,0:T(8,128)(2,1)} %constant.66.clone.refs_2_.refs_4_) | copy-start | bytes 6291460
  17.5 16.8 %collective-permute-start.3 = (bf16[64,4096]{1,0:T(8,128)(2,1)S(1)}, bf16[64,4096]{1,0:T(8,128)(2,1)S(1)}, u32[]{:S(2)}, u32[]{:S(2)}) collective-permute-start(bf16[64,4096]{1,0:T(8,128)(2,1)S(1)} %get-tuple-element.31), channel_id=1, source_target_pairs={{2,0},{3,1},{1,2},{8,3},{6,4},{7,5},{5,6},{12,7},{10,8},{11,9},{9,... | collective-permute-start | bytes 1572872 | tf_op jit(solution)/shard_map/ppermute | solution.py:360
  21.4 18.3 %collective-permute-start.1 = (bf16[64,4096]{1,0:T(8,128)(2,1)S(1)}, bf16[64,4096]{1,0:T(8,128)(2,1)S(1)}, u32[]{:S(2)}, u32[]{:S(2)}) collective-permute-start(bf16[64,4096]{1,0:T(8,128)(2,1)S(1)} %get-tuple-element.32), channel_id=1, source_target_pairs={{4,0},{5,1},{6,2},{7,3},{0,4},{9,5},{2,6},{11,7},{12,8},{13,9},{14... | collective-permute-start | bytes 1572872 | tf_op jit(solution)/shard_map/ppermute | solution.py:360
  34.5 11.4 %collective-permute-start.4 = (bf16[64,4096]{1,0:T(8,128)(2,1)S(1)}, bf16[64,4096]{1,0:T(8,128)(2,1)S(1)}, u32[]{:S(2)}, u32[]{:S(2)}) collective-permute-start(bf16[64,4096]{1,0:T(8,128)(2,1)S(1)} %get-tuple-element.29), channel_id=1, source_target_pairs={{2,0},{3,1},{1,2},{8,3},{6,4},{7,5},{5,6},{12,7},{10,8},{11,9},{9,... | collective-permute-start | bytes 1572872 | tf_op jit(solution)/shard_map/ppermute | solution.py:360
  36.4 20.1 %collective-permute-start.5 = (bf16[64,4096]{1,0:T(8,128)(2,1)S(1)}, bf16[64,4096]{1,0:T(8,128)(2,1)S(1)}, u32[]{:S(2)}, u32[]{:S(2)}) collective-permute-start(bf16[64,4096]{1,0:T(8,128)(2,1)S(1)} %get-tuple-element.28), channel_id=1, source_target_pairs={{4,0},{5,1},{6,2},{7,3},{0,4},{9,5},{2,6},{11,7},{12,8},{13,9},{14... | collective-permute-start | bytes 1572872 | tf_op jit(solution)/shard_map/ppermute | solution.py:360
  45.9 13.4 %copy-start.1 = (bf16[128,256]{1,0:T(8,128)(2,1)S(1)}, bf16[128,256]{1,0:T(8,128)(2,1)}, u32[]{:S(2)}) copy-start(bf16[128,256]{1,0:T(8,128)(2,1)} %constant.70.clone.refs_9_) | copy-start | bytes 196612
  56.5 2.0 %collective-permute-start.6 = (bf16[64,4096]{1,0:T(8,128)(2,1)S(1)}, bf16[64,4096]{1,0:T(8,128)(2,1)S(1)}, u32[]{:S(2)}, u32[]{:S(2)}) collective-permute-start(bf16[64,4096]{1,0:T(8,128)(2,1)S(1)} %collective-permute-done.1.refs_0_), channel_id=1, source_target_pairs={{2,0},{3,1},{0,2},{1,3},{6,4},{7,5},{4,6},{5,7},{10,8},{11,9},{8,1... | collective-permute-start | bytes 1572872 | tf_op jit(solution)/shard_map/ppermute | solution.py:360
  56.6 2.6 %collective-permute-start.7 = (bf16[64,4096]{1,0:T(8,128)(2,1)S(1)}, bf16[64,4096]{1,0:T(8,128)(2,1)S(1)}, u32[]{:S(2)}, u32[]{:S(2)}) collective-permute-start(bf16[64,4096]{1,0:T(8,128)(2,1)S(1)} %collective-permute-done.5.refs_1_), channel_id=1, source_target_pairs={{2,0},{3,1},{0,2},{1,3},{6,4},{7,5},{4,6},{5,7},{10,8},{11,9},{8,1... | collective-permute-start | bytes 1572872 | tf_op jit(solution)/shard_map/ppermute | solution.py:360
